TPU v7x, 32 devices: a whole 2x2x4 slice. The times are simulated.
32 devices in a mesh: atm: 8 (over z, x), ocn: 4 (over y, core).
Axes of the slice: x: 2, y: 2, z: 4, core: 2. Of those that a mesh axis runs over, the one named last changes fastest.
Arguments:
- atm_state: float32 [3, 63, 65536], P(None, None, ('atm', 'ocn')), may hold values from -6 to 6
- diffusivity: float32 [62, 65536], P(None, ('atm', 'ocn')), may hold values from 0.1 to 10
- send_slot: int32 [32, 64], P(('atm', 'ocn')), may hold values from 0 to 127, as said below
- atm_block: int32 [32, 64], P(('atm', 'ocn')), may hold values from 0 to 15
- recv_row: int32 [32, 128], P(('atm', 'ocn')), may hold values from -1 to 31, as said below
- remap_weight: bfloat16 [2048, 128, 128], P(('atm', 'ocn')), may hold values from 0 to 0.0078125
- ocean_tracer: float32 [3, 75, 256, 512], P(None, None, 'atm', 'ocn'), may hold values from -6 to 6
- ocean_velocity: float32 [2, 75, 256, 512], P(None, None, 'atm', 'ocn'), may hold values from -0.24 to 0.24
- exchange_coef: float32 [256, 512], P('atm', 'ocn'), may hold values from 0.2 to 5
- surface_kind: int32 [256, 512], P('atm', 'ocn'), may hold values from 0 to 2
- ice_surface: float32 [3, 256, 512], P(None, 'atm', 'ocn'), may hold values from -6 to 6
Outputs:
- atm_new: float32 [3, 63, 65536], P(None, None, ('atm', 'ocn'))
- ocean_new: float32 [3, 75, 256, 512], P(None, None, 'atm', 'ocn')
Inputs may be any that keep to these rules, and one draw needn't show every extreme that they name: `send_slot`: entry [s, b] = d * 4 + k names owner d and slot k for block b of device s; entries of a row are distinct. Each device sends 4 blocks to itself, and one owner receives 4 blocks from every device. `recv_row`: entry [d, s * 4 + k] is the row of owner d's tile that receives the block that device s sends to slot k of d, and -1 exactly where device s sends nothing to that slot.
All inputs are finite; a program needn't handle non-finite values.
Results may differ from a plain program's by a relative error of at most 0.0003.
Values may be sent and summed in bfloat16 or wider, within the bound.
No kernel may reach another device: no remote copies, remote signals or barrier semaphores. Data moves between devices by JAX's collectives and lax.ppermute only.
A program may use at most 192 MiB of HBM per device.

v0:
```python
import functools

import jax
import jax.numpy as jnp
from jax import lax
from jax.experimental import pallas as pl
from jax.experimental.pallas import tpu as pltpu
from jax.sharding import PartitionSpec as P

NSUB = 4
SUB = 8
LANES = 128
F32 = jnp.float32
BF16 = jnp.bfloat16
VMEM = pl.BlockSpec(memory_space=pltpu.VMEM)
SMEM = pl.BlockSpec(memory_space=pltpu.SMEM)
ANY = pl.BlockSpec(memory_space=pl.ANY)


def shape(dims, kind=F32):
    return jax.ShapeDtypeStruct(dims, kind)


def round_up(value, unit):
    return -(-value // unit) * unit


def params(mib):
    return pltpu.CompilerParams(vmem_limit_bytes=mib * 2**20)


def cost(flops, moved):
    return pl.CostEstimate(flops=int(flops), bytes_accessed=int(moved), transcendentals=0)


def row_pack_kernel(tracer, speed, first, last, head, tail, sem):
    tracer_count, rows, _ = tracer.shape
    speed_count = speed.shape[0]
    total = tracer_count + speed_count
    copies = []
    for place, (start, into) in enumerate(((0, head), (rows - SUB, tail))):
        copies.append(
            pltpu.make_async_copy(
                tracer.at[:, pl.ds(start, SUB), :], into.at[pl.ds(0, tracer_count)], sem.at[place, 0]
            )
        )
        copies.append(
            pltpu.make_async_copy(
                speed.at[:, pl.ds(start, SUB), :],
                into.at[pl.ds(tracer_count, speed_count)],
                sem.at[place, 1],
            )
        )
    for copy in copies:
        copy.start()
    spare = head.shape[0] - total
    for into in (head, tail):
        into[pl.ds(total, spare)] = jnp.zeros((spare, SUB, LANES), F32)
    for copy in copies:
        copy.wait()
    for into, out, shift in ((head, first, 0), (tail, last, SUB - NSUB)):
        flat = into.reshape(into.shape[0] * SUB, LANES)
        for row in range(NSUB):
            for part in range(0, into.shape[0], 16):
                out[row, pl.ds(part, 16), :] = flat[
                    pl.ds(part * SUB + shift + row, 16, stride=SUB), :
                ].astype(BF16)


def row_pack(tracer, speed):
    total = round_up(tracer.shape[0] + speed.shape[0], 16)
    return pl.pallas_call(
        row_pack_kernel,
        out_shape=(shape((NSUB, total, LANES), BF16),) * 2,
        in_specs=[ANY, ANY],
        out_specs=(VMEM, VMEM),
        scratch_shapes=[
            pltpu.VMEM((total, SUB, LANES), F32),
            pltpu.VMEM((total, SUB, LANES), F32),
            pltpu.SemaphoreType.DMA((2, 2)),
        ],
        compiler_params=params(24),
        cost_estimate=cost(1e6, 4e6),
        name="row_pack",
    )(tracer, speed)


def down_kernel(
    profile, diffusion, slots, blocks, weight, coef_c, coef_g, recip, out, prof, diff, placed, total, held, sem
):
    fields, levels, columns = profile.shape
    count = columns // LANES
    width = fields + 1
    block_total = weight.shape[0]
    owners = out.shape[0]
    cap = out.shape[1] // width
    fetch = pltpu.make_async_copy(weight, held, sem)
    fetch.start()
    for field in range(fields):
        for low in range(0, levels, SUB):
            deep = min(SUB, levels - low)
            for block in range(count):
                prof[field, pl.ds(low * count + block, deep, stride=count), :] = profile[
                    field, pl.ds(low, deep), pl.ds(block * LANES, LANES)
                ]
    for low in range(0, levels - 1, SUB):
        deep = min(SUB, levels - 1 - low)
        for block in range(count):
            diff[pl.ds(low * count + block, deep, stride=count), :] = diffusion[
                pl.ds(low, deep), pl.ds(block * LANES, LANES)
            ]
    placed[...] = jnp.zeros(placed.shape, F32)
    total[...] = jnp.zeros(total.shape, F32)
    below = None
    for level in range(levels):
        here = pl.ds(level * count, count)
        rhs = [prof[field, here, :] for field in range(fields)]
        bottom = jnp.full((count, LANES), 1.0, F32)
        if level < levels - 1:
            above = diff[here, :]
            bottom = bottom + above
        if level > 0:
            bottom = bottom + below * (1.0 + c_now)
            rhs = [rhs[field] + below * g_now[field] for field in range(fields)]
        inverse = 1.0 / bottom
        g_now = [value * inverse for value in rhs]
        for field in range(fields):
            coef_g[field, here, :] = g_now[field]
        if level < levels - 1:
            c_now = -above * inverse
            coef_c[here, :] = c_now
            below = above
    recip[...] = inverse
    rows = cap * width
    for slot in range(cap):
        for field, value in enumerate(g_now + [inverse]):
            placed[slot, pl.ds(slot * width + field, count, stride=rows), :] = value
    fetch.wait()
    step = 8

    def body(group, _):
        results = []
        for inner in range(step):
            block = group * step + inner
            slot = slots[0, block]
            start = pl.multiple_of(blocks[0, block] * rows, rows)
            left = placed[slot % cap, pl.ds(start, rows), :].astype(BF16)
            results.append(
                lax.dot_general(
                    left, held[block], (((1,), (1,)), ((), ())), preferred_element_type=F32
                )
            )
        for inner in range(step):
            owner = slots[0, group * step + inner] // cap
            total[owner] = total[owner] + results[inner]
        return 0

    lax.fori_loop(0, block_total // step, body, 0)
    for owner in range(owners):
        out[owner] = total[owner].astype(BF16)


def down(profile, diffusion, slots, blocks, weight, owners, cap):
    fields, levels, columns = profile.shape
    count = columns // LANES
    rows = cap * (fields + 1)
    return pl.pallas_call(
        down_kernel,
        out_shape=(
            shape(((levels - 1) * count, LANES)),
            shape((fields, levels * count, LANES)),
            shape((count, LANES)),
            shape((owners, rows, LANES), BF16),
        ),
        in_specs=[VMEM, VMEM, SMEM, SMEM, ANY],
        out_specs=(VMEM, VMEM, VMEM, VMEM),
        scratch_shapes=[
            pltpu.VMEM((fields, levels * count, LANES), F32),
            pltpu.VMEM(((levels - 1) * count, LANES), F32),
            pltpu.VMEM((cap, count * rows, LANES), F32),
            pltpu.VMEM((owners, rows, LANES), F32),
            pltpu.VMEM(weight.shape, BF16),
            pltpu.SemaphoreType.DMA,
        ],
        compiler_params=params(40),
        cost_estimate=cost(1e7, 6e6),
        name="down_sweep",
    )(profile, diffusion, slots, blocks, weight)


def flux_kernel(arrived, recv, coef, kind, ice, surface, fluxes, answer, *, atm, ocn):
    fields, rows, _ = ice.shape
    width = fields + 1
    slot_total = recv.shape[1]
    chunk = answer.shape[1]
    back = arrived.shape[0] // answer.shape[0]
    spread = (
        lax.broadcasted_iota(jnp.int32, (slot_total, slot_total * width), 1) // width
        == lax.broadcasted_iota(jnp.int32, (slot_total, slot_total * width), 0)
    ).astype(F32).astype(BF16)
    row_of = jnp.broadcast_to(recv[...], (SUB, slot_total)).astype(F32).astype(BF16)
    row_of = jnp.dot(row_of, spread, preferred_element_type=F32)[0:1]
    lane = lax.broadcasted_iota(jnp.int32, (1, slot_total * width), 1)
    key = row_of.astype(jnp.int32) * width + lane % width
    line = lax.broadcasted_iota(jnp.int32, (width * rows, 1), 0)
    chosen = ((line % rows) * width + line // rows == key).astype(F32)
    summed = jnp.dot(chosen.astype(BF16), arrived[...], preferred_element_type=F32)
    hold = jnp.where(kind[...] != 0, coef[...], 0.0)
    over = 1.0 + hold * summed[fields * rows : (fields + 1) * rows]
    rounded = []
    for field in range(fields):
        top = jnp.where(kind[...] == 2, ice[field], surface[field, 0])
        value = hold * (top - summed[field * rows : (field + 1) * rows]) / over
        fluxes[field] = value
        rounded.append(value.astype(BF16).astype(F32))
    stacked = jnp.concatenate(rounded + [jnp.zeros((rows, LANES), F32)], axis=0).astype(BF16)
    turned = chosen.T.astype(BF16)
    returned = jnp.dot(turned, stacked, preferred_element_type=F32)
    answer[:, pl.ds(0, back), :] = returned.astype(BF16).reshape(answer.shape[0], back, LANES)
    answer[:, pl.ds(back, chunk - back), :] = jnp.zeros((answer.shape[0], chunk - back, LANES), BF16)

    source = lax.broadcasted_iota(jnp.int32, (LANES, 3 * LANES), 0)
    target = lax.broadcasted_iota(jnp.int32, (LANES, 3 * LANES), 1)
    own = source + NSUB
    south = source + rows + NSUB
    north = source - (rows - NSUB)
    pos = jnp.where(target < LANES, own, jnp.where(target < 2 * LANES, south, north))
    fits = (
        ((target < LANES) & (source < rows))
        | ((target >= LANES) & (target < 2 * LANES) & (source < NSUB))
        | ((target >= 2 * LANES) & (source >= rows - NSUB) & (source < rows))
    )
    place = (fits & ((pos % SUB) * SUB + pos // SUB == target % LANES)).astype(F32).astype(BF16)
    sides = []
    for field in range(fields):
        tall = jnp.concatenate([rounded[field], jnp.zeros((LANES - rows, LANES), F32)], axis=0)
        sides.append(jnp.dot(tall.T.astype(BF16), place, preferred_element_type=F32))
    blank = jnp.zeros((chunk - back - fields * NSUB, LANES), F32)
    i = lax.axis_index("atm")
    j = lax.axis_index("ocn")
    for di in (-1, 0, 1):
        for dj in (-1, 0, 1):
            if di == 0 and dj == 0:
                continue
            pieces = []
            for field in range(fields):
                if dj == 0:
                    low = 0 if di < 0 else rows - NSUB
                    pieces.append(rounded[field][low : low + NSUB])
                else:
                    low = 0 if dj < 0 else LANES - NSUB
                    part = {0: 0, -1: 1, 1: 2}[di] * LANES
                    pieces.append(sides[field][low : low + NSUB, part : part + LANES])
            tile = jnp.concatenate(pieces + [blank], axis=0).astype(BF16)

            @pl.when((i + di >= 0) & (i + di < atm) & (j + dj >= 0) & (j + dj < ocn))
            def _():
                answer[(i + di) * ocn + j + dj, pl.ds(back, chunk - back), :] = tile


def flux_step(arrived, recv, coef, kind, ice, tracer, owners, atm, ocn):
    fields, rows, _ = ice.shape
    back = arrived.shape[0] // owners
    chunk = back + round_up(fields * NSUB, 16)
    whole = lambda dims: pl.BlockSpec(dims, lambda g: (0,) * len(dims))
    return pl.pallas_call(
        functools.partial(flux_kernel, atm=atm, ocn=ocn),
        grid=(1,),
        out_shape=(shape(ice.shape), shape((owners, chunk, LANES), BF16)),
        in_specs=[
            whole(arrived.shape),
            whole(recv.shape),
            whole(coef.shape),
            whole(kind.shape),
            whole(ice.shape),
            whole((fields, 1, rows, LANES)),
        ],
        out_specs=(whole(ice.shape), whole((owners, chunk, LANES))),
        compiler_params=params(32),
        cost_estimate=cost(1e7, 1e6),
        name="flux_step",
    )(arrived, recv, coef, kind, ice, tracer)


def relayout_kernel(tracer, speed, north, south, out, west, east, raw, tall, done, fetched, stored):
    tracer_count, rows, _ = tracer.shape
    total = tracer_count + speed.shape[0]
    groups = out.shape[0]
    size = total // groups
    high = rows + 2 * NSUB

    def fetch(group):
        here = raw.at[pl.ds(group * size, size)]
        return here, fetched.at[group]

    for group in range(groups):
        into, sem = fetch(group)
        if (group + 1) * size <= tracer_count:
            source = tracer.at[pl.ds(group * size, size)]
        else:
            source = speed.at[pl.ds(group * size - tracer_count, size)]
        pltpu.make_async_copy(source, into, sem).start()
    padded_total = north.shape[1]
    tall[pl.ds(total * high, (padded_total - total) * high), :] = jnp.zeros(
        ((padded_total - total) * high, LANES), F32
    )
    for row in range(NSUB):
        for part in range(0, padded_total, 16):
            for halo, start in ((north, 0), (south, rows + NSUB)):
                tall[pl.ds(part * high + start + row, 16, stride=high), :] = halo[
                    row, pl.ds(part, 16), :
                ].astype(F32)

    def body(group, _):
        into, sem = fetch(group)
        pltpu.make_async_copy(into, into, sem).wait()
        for level in range(size):
            tall[pl.ds(pl.multiple_of(group * size * high, SUB) + level * high + NSUB, rows), :] = raw[
                group * size + level
            ]
        for fine in range(SUB):
            stack = tall[pl.ds(group * size * high + fine, LANES, stride=SUB), :]
            done[group, fine] = stack.T
        pltpu.make_async_copy(done.at[group], out.at[group], stored.at[group]).start()
        return 0

    lax.fori_loop(0, groups, body, 0)
    slabs = groups * SUB
    flat = done.reshape(slabs * LANES, LANES)
    for message, start in ((west, 0), (east, LANES - NSUB)):
        for column in range(NSUB):
            for part in range(0, message.shape[1], 16):
                pieces = []
                for low in (part, part + SUB):
                    if low < slabs:
                        pieces.append(flat[pl.ds(low * LANES + start + column, SUB, stride=LANES), :])
                    else:
                        pieces.append(jnp.zeros((SUB, LANES), F32))
                message[column, pl.ds(part, 16), :] = jnp.concatenate(pieces, axis=0).astype(BF16)
    for group in range(groups):
        pltpu.make_async_copy(done.at[group], out.at[group], stored.at[group]).wait()


def relayout(tracer, speed, north, south, size):
    rows = tracer.shape[1]
    total = tracer.shape[0] + speed.shape[0]
    groups = total // size
    slabs = round_up(groups * SUB, 16)
    return pl.pallas_call(
        relayout_kernel,
        out_shape=(
            shape((groups, SUB, LANES, LANES)),
            shape((NSUB, slabs, LANES), BF16),
            shape((NSUB, slabs, LANES), BF16),
        ),
        in_specs=[ANY, ANY, VMEM, VMEM],
        out_specs=(ANY, VMEM, VMEM),
        scratch_shapes=[
            pltpu.VMEM((total, rows, LANES), F32),
            pltpu.VMEM((north.shape[1] * (rows + 2 * NSUB), LANES), F32),
            pltpu.VMEM((groups, SUB, LANES, LANES), F32),
            pltpu.SemaphoreType.DMA((groups,)),
            pltpu.SemaphoreType.DMA((groups,)),
        ],
        compiler_params=params(48),
        cost_estimate=cost(1e7, 1.4e7),
        name="relayout",
    )(tracer, speed, north, south)


def up_kernel(answered, slots, blocks, weight, coef_c, coef_g, recip, out, held, sums, solved, sem):
    fields, levels, columns = out.shape
    count = columns // LANES
    width = fields + 1
    rows = sums.shape[1]
    cap = rows // width
    fetch = pltpu.make_async_copy(weight, held, sem)
    fetch.start()
    sums[...] = jnp.zeros(sums.shape, F32)
    slot_row = lax.broadcasted_iota(jnp.int32, (rows, LANES), 0) // width
    fetch.wait()
    step = 8

    def body(group, _):
        results = []
        for inner in range(step):
            block = group * step + inner
            left = answered[slots[0, block] // cap, pl.ds(0, rows), :]
            results.append(jnp.dot(left, held[block], preferred_element_type=F32))
        for inner in range(step):
            block = group * step + inner
            kept = jnp.where(slot_row == slots[0, block] % cap, results[inner], 0.0)
            sums[blocks[0, block]] = sums[blocks[0, block]] + kept
        return 0

    lax.fori_loop(0, weight.shape[0] // step, body, 0)
    flat = sums.reshape(count * rows, LANES)
    now = []
    last = pl.ds((levels - 1) * count, count)
    for field in range(fields):
        flux = flat[pl.ds(field, count, stride=rows), :]
        for slot in range(1, cap):
            flux = flux + flat[pl.ds(slot * width + field, count, stride=rows), :]
        now.append(coef_g[field, last, :] + recip[...] * flux)
        solved[field, last, :] = now[field]
    for level in range(levels - 2, -1, -1):
        here = pl.ds(level * count, count)
        for field in range(fields):
            now[field] = coef_g[field, here, :] - coef_c[here, :] * now[field]
            solved[field, here, :] = now[field]
    for field in range(fields):
        for low in range(0, levels, SUB):
            deep = min(SUB, levels - low)
            for block in range(count):
                out[field, pl.ds(low, deep), pl.ds(block * LANES, LANES)] = solved[
                    field, pl.ds(low * count + block, deep, stride=count), :
                ]


def up(answered, slots, blocks, weight, coef_c, coef_g, recip, levels, cap):
    fields = coef_g.shape[0]
    count = recip.shape[0]
    rows = cap * (fields + 1)
    return pl.pallas_call(
        up_kernel,
        out_shape=shape((fields, levels, count * LANES)),
        in_specs=[VMEM, SMEM, SMEM, ANY, VMEM, VMEM, VMEM],
        out_specs=VMEM,
        scratch_shapes=[
            pltpu.VMEM(weight.shape, BF16),
            pltpu.VMEM((count, rows, LANES), F32),
            pltpu.VMEM((fields, levels * count, LANES), F32),
            pltpu.SemaphoreType.DMA,
        ],
        compiler_params=params(40),
        cost_estimate=cost(1e7, 6e6),
        name="up_sweep",
    )(answered, slots, blocks, weight, coef_c, coef_g, recip)


def advect_kernel(
    laid, from_west, from_east, fluxes, answered, out, here, there, speed, coef, thin, halo, high, raw, fetched, stored,
    *, fields, atm, ocn
):
    groups = laid.shape[0]
    per = groups // (fields + 2)
    size = out.shape[0] // (fields * per)
    rows = out.shape[1]
    tall = rows + 2 * NSUB
    wide = here.shape[2]
    tiles = wide // SUB
    back = answered.shape[1] - round_up(fields * NSUB, 16)

    def fetch(group):
        if group < fields * per:
            into = here.at[group, :, pl.ds(SUB, LANES), :]
        else:
            into = speed.at[group - fields * per, :, pl.ds(SUB, LANES), :]
        return pltpu.make_async_copy(laid.at[group], into, fetched.at[group])

    for group in range(groups):
        fetch(group).start()
    for ref in (here, speed):
        ref[:, :, pl.ds(0, SUB), :] = jnp.zeros(ref.shape[:2] + (SUB, LANES), F32)
        ref[:, :, pl.ds(wide - SUB, SUB), :] = jnp.zeros(ref.shape[:2] + (SUB, LANES), F32)
    for side, message, start in ((0, from_west, SUB - NSUB), (1, from_east, wide - SUB)):
        for column in range(NSUB):
            halo[...] = message[column].astype(F32)
            for group in range(groups):
                ref, at = (here, group) if group < fields * per else (speed, group - fields * per)
                flat = ref.reshape(ref.shape[0] * SUB * wide, LANES)
                flat[pl.ds(at * SUB * wide + start + column, SUB, stride=wide), :] = halo[
                    pl.ds(group * SUB, SUB), :
                ]
    i = lax.axis_index("atm")
    j = lax.axis_index("ocn")

    def neighbour(di, dj):
        inside = (i + di >= 0) & (i + di < atm) & (j + dj >= 0) & (j + dj < ocn)
        index = jnp.where(inside, (i + di) * ocn + j + dj, 0)
        value = answered[index, pl.ds(back, answered.shape[1] - back), :].astype(F32)
        return jnp.where(inside, value, 0.0)

    up_rows = neighbour(-1, 0)
    down_rows = neighbour(1, 0)
    thin[...] = jnp.zeros(thin.shape, F32)
    for field in range(fields):
        thin[field, pl.ds(0, NSUB), :] = up_rows[field * NSUB : (field + 1) * NSUB]
        thin[field, pl.ds(NSUB, rows), :] = fluxes[field]
        thin[field, pl.ds(NSUB + rows, NSUB), :] = down_rows[field * NSUB : (field + 1) * NSUB]
    for field in range(fields):
        fetch(field * per).wait()
        for fine in range(SUB):
            few = thin[field, pl.ds(fine, SUB, stride=SUB), :]
            stack = jnp.concatenate([few, jnp.zeros((LANES - SUB, LANES), F32)], axis=0)
            at = (field * per, fine, pl.ds(SUB, LANES))
            here[at] = here[at] - stack.T
    lane = lax.broadcasted_iota(jnp.int32, (16, LANES), 1)
    for dj, start in ((-1, SUB - NSUB), (1, wide - SUB)):
        side = neighbour(-1, dj) + neighbour(0, dj) + neighbour(1, dj)
        for fine in range(SUB):
            moved = side if fine == 0 else pltpu.roll(side, LANES - SUB * fine, 1)
            moved = jnp.where(lane < SUB, moved, 0.0)
            for field in range(fields):
                at = (field * per, fine, pl.ds(start, NSUB))
                here[at] = here[at] - moved[field * NSUB : (field + 1) * NSUB]

    def shifted(ref, lead, tile, base, value, side):
        if side < 0:
            if isinstance(tile, int) and tile == 0:
                return pltpu.roll(value, 1, 0)
            return ref[lead + (pl.ds(base - 1, SUB),)]
        if isinstance(tile, int) and tile == tiles - 1:
            return pltpu.roll(value, SUB - 1, 0)
        return ref[lead + (pl.ds(base + 1, SUB),)]

    def coefs(group, tile):
        base = tile * SUB if isinstance(tile, int) else pl.multiple_of(tile * SUB, SUB)
        at = pl.ds(base, SUB)
        along = [speed[group, fine, at, :] for fine in range(SUB)]
        along.append(pltpu.roll(along[0], LANES - 1, 1))
        faces = [0.5 * (along[fine] + along[fine + 1]) for fine in range(SUB)]
        gain = [jnp.maximum(face, 0.0) for face in faces]
        lose = [gain[fine] - faces[fine] for fine in range(SUB)]
        gain_low = [pltpu.roll(gain[-1], 1, 1)] + gain[:-1]
        lose_low = [pltpu.roll(lose[-1], 1, 1)] + lose[:-1]
        for fine in range(SUB):
            lead = (per + group, fine)
            value = speed[lead + (at,)]
            above = 0.5 * (value + shifted(speed, lead, tile, base, value, 1))
            under = 0.5 * (value + shifted(speed, lead, tile, base, value, -1))
            gain_above = jnp.maximum(above, 0.0)
            gain_under = jnp.maximum(under, 0.0)
            lose_under = gain_under - under
            coef[0, fine, at, :] = 1.0 - (gain[fine] + lose_low[fine] + gain_above + lose_under)
            coef[1, fine, at, :] = gain_low[fine]
            coef[2, fine, at, :] = lose[fine]
            coef[3, fine, at, :] = gain_under
            coef[4, fine, at, :] = gain_above - above

    def update(group, src, dst, tile):
        base = tile * SUB if isinstance(tile, int) else pl.multiple_of(tile * SUB, SUB)
        at = pl.ds(base, SUB)
        lead = [src[0](field, group) for field in range(fields)]
        goal = [dst[0](field, group) for field in range(fields)]
        values = [[src[1][lead[f], fine, at, :] for fine in range(SUB)] for f in range(fields)]
        for fine in range(SUB):
            own, low, high_c, left, right = [coef[part, fine, at, :] for part in range(5)]
            for field in range(fields):
                value = values[field][fine]
                prior = values[field][fine - 1] if fine > 0 else pltpu.roll(values[field][-1], 1, 1)
                after = (
                    values[field][fine + 1]
                    if fine < SUB - 1
                    else pltpu.roll(values[field][0], LANES - 1, 1)
                )
                index = (lead[field], fine)
                before = shifted(src[1], index, tile, base, value, -1)
                behind = shifted(src[1], index, tile, base, value, 1)
                dst[1][goal[field], fine, at, :] = (
                    own * value + low * prior + high_c * after + left * before + right * behind
                )

    def sweep(work, edges):
        if edges:
            work(0)
            work(tiles - 1)
        lax.fori_loop(1, tiles - 1, lambda tile, _: (work(tile), 0)[1], 0, unroll=4)

    def body(group, _):
        for field in range(fields):
            at = field * per + group

            @pl.when(group > 0)
            def _():
                pltpu.make_async_copy(
                    laid.at[at], here.at[at, :, pl.ds(SUB, LANES), :], fetched.at[at]
                ).wait()

        for part in range(2):
            at = part * per + group
            pltpu.make_async_copy(
                laid.at[fields * per + at],
                speed.at[at, :, pl.ds(SUB, LANES), :],
                fetched.at[fields * per + at],
            ).wait()
        sweep(functools.partial(coefs, group), True)
        first = (lambda field, group: field * per + group, here)
        second = (lambda field, group: field, there)
        for substep in range(NSUB):
            src, dst = (first, second) if substep % 2 == 0 else (second, first)
            sweep(functools.partial(update, group, src, dst), substep < NSUB - 1)
        for field in range(fields):
            lead = field * per + group
            for fine in range(SUB):
                turned = here[lead, fine, pl.ds(SUB, LANES), :].T
                high[pl.ds(fine, LANES, stride=SUB), :] = turned
            base = lead * size
            for level in range(size):
                raw[base + level] = high[pl.ds(level * tall + NSUB, rows), :]
            pltpu.make_async_copy(
                raw.at[pl.ds(base, size)], out.at[pl.ds(base, size)], stored.at[lead]
            ).start()
        return 0

    lax.fori_loop(0, per, body, 0)
    for lead in range(fields * per):
        pltpu.make_async_copy(
            raw.at[pl.ds(lead * size, size)], out.at[pl.ds(lead * size, size)], stored.at[lead]
        ).wait()


def advect(laid, from_west, from_east, fluxes, answered, rows, size, atm, ocn):
    fields = fluxes.shape[0]
    groups = laid.shape[0]
    per = groups // (fields + 2)
    wide = LANES + 2 * SUB
    total = fields * per * size
    return pl.pallas_call(
        functools.partial(advect_kernel, fields=fields, atm=atm, ocn=ocn),
        out_shape=shape((total, rows, LANES)),
        in_specs=[ANY, VMEM, VMEM, VMEM, VMEM],
        out_specs=ANY,
        scratch_shapes=[
            pltpu.VMEM((fields * per, SUB, wide, LANES), F32),
            pltpu.VMEM((fields, SUB, wide, LANES), F32),
            pltpu.VMEM((2 * per, SUB, wide, LANES), F32),
            pltpu.VMEM((5, SUB, wide, LANES), F32),
            pltpu.VMEM((fields, SUB * SUB, LANES), F32),
            pltpu.VMEM((from_west.shape[1], LANES), F32),
            pltpu.VMEM((SUB * LANES, LANES), F32),
            pltpu.VMEM((total, rows, LANES), F32),
            pltpu.SemaphoreType.DMA((groups,)),
            pltpu.SemaphoreType.DMA((fields * per,)),
        ],
        compiler_params=params(48),
        cost_estimate=cost(5e7, 1.2e7),
        name="advect",
    )(laid, from_west, from_east, fluxes, answered)


def per_device(
    atm_state,
    diffusivity,
    send_slot,
    atm_block,
    recv_row,
    remap_weight,
    ocean_tracer,
    ocean_velocity,
    exchange_coef,
    surface_kind,
    ice_surface,
):
    atm, ocn = lax.axis_size("atm"), lax.axis_size("ocn")
    owners = atm * ocn
    fields, levels, _ = atm_state.shape
    cap = recv_row.shape[1] // owners
    depth, rows, columns = ocean_tracer.shape[1:]
    most = LANES // ((rows + 2 * NSUB) // SUB)
    size = max(count for count in range(1, most + 1) if depth % count == 0)
    tracer = ocean_tracer.reshape(-1, rows, columns)
    speed = ocean_velocity.reshape(-1, rows, columns)

    def neighbours(axis):
        count = lax.axis_size(axis)
        up = [(place, place + 1) for place in range(count - 1)]
        return up, [(target, source) for source, target in up]

    forward, backward = neighbours("atm")
    first, last = row_pack(tracer, speed)
    south = lax.ppermute(first, "atm", backward)
    north = lax.ppermute(last, "atm", forward)
    coef_c, coef_g, recip, outgoing = down(
        atm_state, diffusivity, send_slot, atm_block, remap_weight, owners, cap
    )
    arrived = lax.all_to_all(outgoing, ("atm", "ocn"), split_axis=0, concat_axis=0, tiled=True)
    fluxes, answer = flux_step(
        arrived.reshape(-1, LANES), recv_row, exchange_coef, surface_kind, ice_surface,
        ocean_tracer, owners, atm, ocn,
    )
    answered = lax.all_to_all(answer, ("atm", "ocn"), split_axis=0, concat_axis=0, tiled=True)
    laid, to_west, to_east = relayout(tracer, speed, north, south, size)
    forward, backward = neighbours("ocn")
    from_east = lax.ppermute(to_west, "ocn", backward)
    from_west = lax.ppermute(to_east, "ocn", forward)
    atm_new = up(
        answered, send_slot, atm_block, remap_weight, coef_c, coef_g, recip, levels, cap
    )
    ocean_new = advect(laid, from_west, from_east, fluxes, answered, rows, size, atm, ocn)
    return atm_new, ocean_new.reshape(ocean_tracer.shape)


def solution(mesh):
    placed = (
        P(None, None, ("atm", "ocn")),
        P(None, ("atm", "ocn")),
        P(("atm", "ocn"), None),
        P(("atm", "ocn"), None),
        P(("atm", "ocn"), None),
        P(("atm", "ocn"), None, None),
        P(None, None, "atm", "ocn"),
        P(None, None, "atm", "ocn"),
        P("atm", "ocn"),
        P("atm", "ocn"),
        P(None, "atm", "ocn"),
    )
    return jax.shard_map(
        per_device,
        mesh=mesh,
        in_specs=placed,
        out_specs=(P(None, None, ("atm", "ocn")), P(None, None, "atm", "ocn")),
        check_vma=False,
    )
```

profile of v0, /device:TPU:1, one launch (start us, length us, event | category | flops | bytes accessed | tf_op | source)
XLA Modules:
  0.0 81.6 jit_solution(12968940892835425192)
XLA Ops:
  0.6 0.0 copy-start.2
  0.6 0.0 copy-start.3
  0.7 1.7 %copy-done.3 = bf16[64,128,128]{2,1,0:T(8,128)(2,1)S(1)} copy-done((bf16[64,128,128]{2,1,0:T(8,128)(2,1)S(1)}, bf16[64,128,128]{2,1,0:T(8,128)(2,1)}, u32[]{:S(2)}) %copy-start.3) | copy-done | bytes 2097176
  2.4 0.0 copy-start.5
  2.4 1.4 %copy-done.5 = f32[3,63,2048]{2,1,0:T(8,128)S(1)} copy-done((f32[3,63,2048]{2,1,0:T(8,128)S(1)}, f32[3,63,2048]{2,1,0:T(8,128)}, u32[]{:S(2)}) %copy-start.5) | copy-done | bytes 1548312
  3.8 0.0 copy-start.8
  3.8 1.0 %copy-done.8 = f32[62,2048]{1,0:T(8,128)S(1)} copy-done((f32[62,2048]{1,0:T(8,128)S(1)}, f32[62,2048]{1,0:T(8,128)}, u32[]{:S(2)}) %copy-start.8) | copy-done | bytes 507928
  4.8 0.0 copy-start.12
  4.8 0.7 copy-done.12
  5.5 0.0 copy-start.14
  5.5 0.7 copy-done.14
  6.1 4.7 %down_sweep.1 = (f32[992,128]{1,0:T(8,128)S(1)}, f32[3,1008,128]{2,1,0:T(8,128)S(1)}, f32[16,128]{1,0:T(8,128)S(1)}, bf16[32,16,128]{2,1,0:T(8,128)(2,1)}) custom-call(f32[3,63,2048]{2,1,0:T(8,128)S(1)} %copy-done.5, f32[62,2048]{1,0:T(8,128)S(1)} %copy-done.8, s32[1,64]{1,0:T(1,128)S(1)} %copy-done.12, s32[1,64]{1,0:T(1,128)S(1)} %copy-done.14, ...), custom_call_target="tpu_custom_call" | custom-call | flops 10000000 | bytes 6000000 | tf_op jit(solution)/shard_map/down_sweep/pallas_call | solution.py:167
  10.9 0.0 copy-start.6
  10.9 1.1 %copy-done.6 = f32[3,1008,128]{2,1,0:T(8,128)} copy-done((f32[3,1008,128]{2,1,0:T(8,128)}, f32[3,1008,128]{2,1,0:T(8,128)S(1)}, u32[]{:S(2)}) %copy-start.6) | copy-done | bytes 1548312
  12.0 7.1 %all-to-all-start = ((bf16[32,16,128]{2,1,0:T(8,128)(2,1)}), bf16[32,16,128]{2,1,0:T(8,128)(2,1)S(1)}, u32[]{:S(2)}, u32[]{:S(2)}) async-start(bf16[32,16,128]{2,1,0:T(8,128)(2,1)} %get-tuple-element.13), calls=%async_computation | async-start | bytes 262144 | tf_op jit(solution)/shard_map/all_to_all | solution.py:677
  19.1 0.0 copy-done.2
  19.1 0.0 copy-start
  19.1 2.0 %copy-done = f32[3,75,32,128]{3,2,1,0:T(8,128)S(1)} copy-done((f32[3,75,32,128]{3,2,1,0:T(8,128)S(1)}, f32[3,75,32,128]{3,2,1,0:T(8,128)}, u32[]{:S(2)}) %copy-start) | copy-done | bytes 3686424
  21.2 0.0 copy-start.9
  21.2 0.0 copy-start.10
  21.2 0.0 copy-start.11
  21.2 0.0 copy-start.16
  21.2 1.5 %row_pack.1 = (bf16[4,384,128]{2,1,0:T(8,128)(2,1)}, bf16[4,384,128]{2,1,0:T(8,128)(2,1)}) custom-call(f32[225,32,128]{2,1,0:T(8,128)S(1)} %bitcast.5, f32[150,32,128]{2,1,0:T(8,128)S(1)} %bitcast.6), custom_call_target="tpu_custom_call" | custom-call | flops 1000000 | bytes 4000000 | tf_op jit(solution)/shard_map/row_pack/pallas_call | solution.py:72
  22.7 4.1 %collective-permute-start = (bf16[4,384,128]{2,1,0:T(8,128)(2,1)}, bf16[4,384,128]{2,1,0:T(8,128)(2,1)}, u32[]{:S(2)}, u32[]{:S(2)}) collective-permute-start(bf16[4,384,128]{2,1,0:T(8,128)(2,1)} %get-tuple-element.18), channel_id=1, source_target_pairs={{0,4},{4,8},{8,12},{12,16},{16,20},{20,24},{24,28},{1,5},{5,9},{9,... | collective-permute-start | bytes 1179656 | tf_op jit(solution)/shard_map/ppermute | solution.py:673
  26.8 1.3 %collective-permute-start.1 = (bf16[4,384,128]{2,1,0:T(8,128)(2,1)}, bf16[4,384,128]{2,1,0:T(8,128)(2,1)}, u32[]{:S(2)}, u32[]{:S(2)}) collective-permute-start(bf16[4,384,128]{2,1,0:T(8,128)(2,1)} %get-tuple-element.19), channel_id=1, source_target_pairs={{4,0},{8,4},{12,8},{16,12},{20,16},{24,20},{28,24},{5,1},{9,5},{13... | collective-permute-start | bytes 1179656 | tf_op jit(solution)/shard_map/ppermute | solution.py:672
  28.1 0.0 all-to-all-done
  28.1 0.0 copy-done.9
  28.1 0.0 copy-done.10
  28.1 0.0 copy-done.11
  28.1 0.0 copy-done.16
  28.1 0.0 copy-start.1
  28.1 2.0 %copy-done.1 = f32[3,75,32,128]{3,2,1,0:T(8,128)S(1)} copy-done((f32[3,75,32,128]{3,2,1,0:T(8,128)S(1)}, f32[3,75,32,128]{3,2,1,0:T(8,128)}, u32[]{:S(2)}) %copy-start.1) | copy-done | bytes 3686424
  30.2 1.4 %flux_step.1 = (f32[3,32,128]{2,1,0:T(8,128)S(1)}, bf16[32,32,128]{2,1,0:T(8,128)(2,1)}) custom-call(bf16[512,128]{1,0:T(8,128)(2,1)S(1)} %bitcast.8, s32[1,128]{1,0:T(1,128)S(1)} %copy-done.16, f32[32,128]{1,0:T(8,128)S(1)} %copy-done.10, s32[32,128]{1,0:T(8,128)S(1)} %copy-done.11, f32[3,32,128]{2,1,0:T(8,128)S(1)} %copy-done.9, ...), custom_call_target="tpu_custom_call" | custom-call | flops 10000000 | bytes 1000000 | tf_op jit(solution)/shard_map/flux_step/pallas_call | solution.py:266
  31.6 7.1 %all-to-all-start.1 = ((bf16[32,32,128]{2,1,0:T(8,128)(2,1)}), bf16[32,32,128]{2,1,0:T(8,128)(2,1)S(1)}, u32[]{:S(2)}, u32[]{:S(2)}) async-start(bf16[32,32,128]{2,1,0:T(8,128)(2,1)} %get-tuple-element.14), calls=%async_computation.1 | async-start | bytes 524288 | tf_op jit(solution)/shard_map/all_to_all | solution.py:682
  38.7 0.0 copy-start.13
  38.7 0.0 copy-start.15
  38.7 5.4 %collective-permute-done.north = bf16[4,384,128]{2,1,0:T(8,128)(2,1)} collective-permute-done((bf16[4,384,128]{2,1,0:T(8,128)(2,1)}, bf16[4,384,128]{2,1,0:T(8,128)(2,1)}, u32[]{:S(2)}, u32[]{:S(2)}) %collective-permute-start) | collective-permute-done | bytes 393248 | tf_op jit(solution)/shard_map/ppermute | solution.py:673
  44.1 0.0 collective-permute-done.1.south
  44.1 7.1 %relayout.1 = (f32[15,8,128,128]{3,2,1,0:T(8,128)}, bf16[4,128,128]{2,1,0:T(8,128)(2,1)S(1)}, bf16[4,128,128]{2,1,0:T(8,128)(2,1)S(1)}) custom-call(f32[225,32,128]{2,1,0:T(8,128)} %bitcast.4, f32[150,32,128]{2,1,0:T(8,128)S(1)} %bitcast.7, bf16[4,384,128]{2,1,0:T(8,128)(2,1)} %collective-permute-done.north, bf16[4,384,128]{2,1,0:T(8,128)(2,1)} %collective-permute-done.1.south), custom_call_target="tpu_custom_call" | custom-call | flops 10000000 | bytes 14000000 | tf_op jit(solution)/shard_map/relayout/pallas_call | solution.py:349
  51.3 5.0 %collective-permute-start.2 = (bf16[4,128,128]{2,1,0:T(8,128)(2,1)S(1)}, bf16[4,128,128]{2,1,0:T(8,128)(2,1)S(1)}, u32[]{:S(2)}, u32[]{:S(2)}) collective-permute-start(bf16[4,128,128]{2,1,0:T(8,128)(2,1)S(1)} %get-tuple-element.21), channel_id=1, source_target_pairs={{0,1},{1,2},{2,3},{4,5},{5,6},{6,7},{8,9},{9,10},{10,11},{12,13},{... | collective-permute-start | bytes 393224 | tf_op jit(solution)/shard_map/ppermute | solution.py:686
  56.3 1.9 %collective-permute-start.3 = (bf16[4,128,128]{2,1,0:T(8,128)(2,1)S(1)}, bf16[4,128,128]{2,1,0:T(8,128)(2,1)S(1)}, u32[]{:S(2)}, u32[]{:S(2)}) collective-permute-start(bf16[4,128,128]{2,1,0:T(8,128)(2,1)S(1)} %get-tuple-element.22), channel_id=1, source_target_pairs={{1,0},{2,1},{3,2},{5,4},{6,5},{7,6},{9,8},{10,9},{11,10},{13,12},{... | collective-permute-start | bytes 393224 | tf_op jit(solution)/shard_map/ppermute | solution.py:685
  58.3 0.0 all-to-all-done.1.answered
  58.3 0.0 copy-done.13
  58.3 0.0 copy-done.15
  58.3 0.0 copy-start.4
  58.3 1.6 %copy-done.4 = bf16[64,128,128]{2,1,0:T(8,128)(2,1)S(1)} copy-done((bf16[64,128,128]{2,1,0:T(8,128)(2,1)S(1)}, bf16[64,128,128]{2,1,0:T(8,128)(2,1)}, u32[]{:S(2)}) %copy-start.4) | copy-done | bytes 2097176
  59.9 0.0 copy-start.7
  59.9 1.4 %copy-done.7 = f32[3,1008,128]{2,1,0:T(8,128)S(1)} copy-done((f32[3,1008,128]{2,1,0:T(8,128)S(1)}, f32[3,1008,128]{2,1,0:T(8,128)}, u32[]{:S(2)}) %copy-start.7) | copy-done | bytes 1548312
  61.3 4.0 %up_sweep.1 = f32[3,63,2048]{2,1,0:T(8,128)} custom-call(bf16[32,32,128]{2,1,0:T(8,128)(2,1)S(1)} %all-to-all-done.1.answered, s32[1,64]{1,0:T(1,128)S(1)} %copy-done.13, s32[1,64]{1,0:T(1,128)S(1)} %copy-done.15, bf16[64,128,128]{2,1,0:T(8,128)(2,1)S(1)} %copy-done.4, f32[992,128]{1,0:T(8,128)S(1)} %get-tuple-element.15.coef_c, ...), custom_call_target="tpu_custom_call" | custom-call | flops 10000000 | bytes 6000000 | tf_op jit(solution)/shard_map/up_sweep/pallas_call | solution.py:424
  65.3 0.0 collective-permute-done.2.from_west
  65.3 0.0 collective-permute-done.3.from_east
  65.3 16.2 %advect.1 = f32[225,32,128]{2,1,0:T(8,128)} custom-call(f32[15,8,128,128]{3,2,1,0:T(8,128)} %get-tuple-element.20.laid, bf16[4,128,128]{2,1,0:T(8,128)(2,1)S(1)} %collective-permute-done.2.from_west, bf16[4,128,128]{2,1,0:T(8,128)(2,1)S(1)} %collective-permute-done.3.from_east, f32[3,32,128]{2,1,0:T(8,128)S(1)} %get-tuple-element.23.fluxes, ...), custom_call_target="tpu_custom_call" | custom-call | flops 50000000 | bytes 12000000 | tf_op jit(solution)/shard_map/advect/pallas_call | solution.py:619
Async XLA Ops:
  0.6 18.5 %copy-start.2 = (f32[2,75,32,128]{3,2,1,0:T(8,128)S(1)}, f32[2,75,32,128]{3,2,1,0:T(8,128)}, u32[]{:S(2)}) copy-start(f32[2,75,32,128]{3,2,1,0:T(8,128)} %param.18) | copy-start | bytes 7372804
  0.6 1.7 %copy-start.3 = (bf16[64,128,128]{2,1,0:T(8,128)(2,1)S(1)}, bf16[64,128,128]{2,1,0:T(8,128)(2,1)}, u32[]{:S(2)}) copy-start(bf16[64,128,128]{2,1,0:T(8,128)(2,1)} %weight.3) | copy-start | bytes 6291460
  2.4 1.4 %copy-start.5 = (f32[3,63,2048]{2,1,0:T(8,128)S(1)}, f32[3,63,2048]{2,1,0:T(8,128)}, u32[]{:S(2)}) copy-start(f32[3,63,2048]{2,1,0:T(8,128)} %profile.1) | copy-start | bytes 4644868
  3.8 1.0 %copy-start.8 = (f32[62,2048]{1,0:T(8,128)S(1)}, f32[62,2048]{1,0:T(8,128)}, u32[]{:S(2)}) copy-start(f32[62,2048]{1,0:T(8,128)} %diffusion.1) | copy-start | bytes 1523716
  4.8 0.7 copy-start.12
  5.5 0.7 copy-start.14
  10.9 1.1 %copy-start.6 = (f32[3,1008,128]{2,1,0:T(8,128)}, f32[3,1008,128]{2,1,0:T(8,128)S(1)}, u32[]{:S(2)}) copy-start(f32[3,1008,128]{2,1,0:T(8,128)S(1)} %get-tuple-element.16.coef_g) | copy-start | bytes 4644868
  12.0 16.1 %all-to-all-start = ((bf16[32,16,128]{2,1,0:T(8,128)(2,1)}), bf16[32,16,128]{2,1,0:T(8,128)(2,1)S(1)}, u32[]{:S(2)}, u32[]{:S(2)}) async-start(bf16[32,16,128]{2,1,0:T(8,128)(2,1)} %get-tuple-element.13), calls=%async_computation | async-start | bytes 262144 | tf_op jit(solution)/shard_map/all_to_all | solution.py:677
  19.1 2.0 %copy-start = (f32[3,75,32,128]{3,2,1,0:T(8,128)S(1)}, f32[3,75,32,128]{3,2,1,0:T(8,128)}, u32[]{:S(2)}) copy-start(f32[3,75,32,128]{3,2,1,0:T(8,128)} %surface.1) | copy-start | bytes 11059204
  21.2 6.9 %copy-start.9 = (f32[3,32,128]{2,1,0:T(8,128)S(1)}, f32[3,32,128]{2,1,0:T(8,128)}, u32[]{:S(2)}) copy-start(f32[3,32,128]{2,1,0:T(8,128)} %ice.1) | copy-start | bytes 147460
  21.2 6.9 %copy-start.10 = (f32[32,128]{1,0:T(8,128)S(1)}, f32[32,128]{1,0:T(8,128)}, u32[]{:S(2)}) copy-start(f32[32,128]{1,0:T(8,128)} %coef.1) | copy-start | bytes 49156
  21.2 6.9 %copy-start.11 = (s32[32,128]{1,0:T(8,128)S(1)}, s32[32,128]{1,0:T(8,128)}, u32[]{:S(2)}) copy-start(s32[32,128]{1,0:T(8,128)} %kind.1) | copy-start | bytes 49156
  21.2 6.9 %copy-start.16 = (s32[1,128]{1,0:T(1,128)S(1)}, s32[1,128]{1,0:T(1,128)}, u32[]{:S(2)}) copy-start(s32[1,128]{1,0:T(1,128)} %recv.1) | copy-start | bytes 1540
  22.7 21.4 %collective-permute-start = (bf16[4,384,128]{2,1,0:T(8,128)(2,1)}, bf16[4,384,128]{2,1,0:T(8,128)(2,1)}, u32[]{:S(2)}, u32[]{:S(2)}) collective-permute-start(bf16[4,384,128]{2,1,0:T(8,128)(2,1)} %get-tuple-element.18), channel_id=1, source_target_pairs={{0,4},{4,8},{8,12},{12,16},{16,20},{20,24},{24,28},{1,5},{5,9},{9,... | collective-permute-start | bytes 1179656 | tf_op jit(solution)/shard_map/ppermute | solution.py:673
  26.8 17.4 %collective-permute-start.1 = (bf16[4,384,128]{2,1,0:T(8,128)(2,1)}, bf16[4,384,128]{2,1,0:T(8,128)(2,1)}, u32[]{:S(2)}, u32[]{:S(2)}) collective-permute-start(bf16[4,384,128]{2,1,0:T(8,128)(2,1)} %get-tuple-element.19), channel_id=1, source_target_pairs={{4,0},{8,4},{12,8},{16,12},{20,16},{24,20},{28,24},{5,1},{9,5},{13... | collective-permute-start | bytes 1179656 | tf_op jit(solution)/shard_map/ppermute | solution.py:672
  28.1 2.0 %copy-start.1 = (f32[3,75,32,128]{3,2,1,0:T(8,128)S(1)}, f32[3,75,32,128]{3,2,1,0:T(8,128)}, u32[]{:S(2)}) copy-start(f32[3,75,32,128]{3,2,1,0:T(8,128)} %surface.1) | copy-start | bytes 11059204
  31.6 26.7 %all-to-all-start.1 = ((bf16[32,32,128]{2,1,0:T(8,128)(2,1)}), bf16[32,32,128]{2,1,0:T(8,128)(2,1)S(1)}, u32[]{:S(2)}, u32[]{:S(2)}) async-start(bf16[32,32,128]{2,1,0:T(8,128)(2,1)} %get-tuple-element.14), calls=%async_computation.1 | async-start | bytes 524288 | tf_op jit(solution)/shard_map/all_to_all | solution.py:682
  38.7 19.6 %copy-start.13 = (s32[1,64]{1,0:T(1,128)S(1)}, s32[1,64]{1,0:T(1,128)}, u32[]{:S(2)}) copy-start(s32[1,64]{1,0:T(1,128)} %slots.3) | copy-start | bytes 772
  38.7 19.6 %copy-start.15 = (s32[1,64]{1,0:T(1,128)S(1)}, s32[1,64]{1,0:T(1,128)}, u32[]{:S(2)}) copy-start(s32[1,64]{1,0:T(1,128)} %blocks.3) | copy-start | bytes 772
  51.3 14.0 %collective-permute-start.2 = (bf16[4,128,128]{2,1,0:T(8,128)(2,1)S(1)}, bf16[4,128,128]{2,1,0:T(8,128)(2,1)S(1)}, u32[]{:S(2)}, u32[]{:S(2)}) collective-permute-start(bf16[4,128,128]{2,1,0:T(8,128)(2,1)S(1)} %get-tuple-element.21), channel_id=1, source_target_pairs={{0,1},{1,2},{2,3},{4,5},{5,6},{6,7},{8,9},{9,10},{10,11},{12,13},{... | collective-permute-start | bytes 393224 | tf_op jit(solution)/shard_map/ppermute | solution.py:686
  56.3 9.0 %collective-permute-start.3 = (bf16[4,128,128]{2,1,0:T(8,128)(2,1)S(1)}, bf16[4,128,128]{2,1,0:T(8,128)(2,1)S(1)}, u32[]{:S(2)}, u32[]{:S(2)}) collective-permute-start(bf16[4,128,128]{2,1,0:T(8,128)(2,1)S(1)} %get-tuple-element.22), channel_id=1, source_target_pairs={{1,0},{2,1},{3,2},{5,4},{6,5},{7,6},{9,8},{10,9},{11,10},{13,12},{... | collective-permute-start | bytes 393224 | tf_op jit(solution)/shard_map/ppermute | solution.py:685
  58.3 1.6 %copy-start.4 = (bf16[64,128,128]{2,1,0:T(8,128)(2,1)S(1)}, bf16[64,128,128]{2,1,0:T(8,128)(2,1)}, u32[]{:S(2)}) copy-start(bf16[64,128,128]{2,1,0:T(8,128)(2,1)} %weight.3) | copy-start | bytes 6291460
  59.9 1.4 %copy-start.7 = (f32[3,1008,128]{2,1,0:T(8,128)S(1)}, f32[3,1008,128]{2,1,0:T(8,128)}, u32[]{:S(2)}) copy-start(f32[3,1008,128]{2,1,0:T(8,128)} %copy-done.6) | copy-start | bytes 4644868
where the time goes:
time: 83.1 us; the launch traced here: 81.6 us
  Pallas kernels  35 us (42%)
  starting transfers between devices  26.5 us (32%)
  local copies, waits for them, and re-layouts  13.7 us (16%)
  waiting for transfers between devices  5.46 us (7%)
  between operations  0.87 us (1%)
    pallas_call x1, Pallas kernels, advect(): pl.pallas_call(functools.partial(advect_kernel, fields=fields, atm=atm, o...  16.2 us
    unnamed x34, local copies, waits for them, and re-layouts  13.7 us
    pallas_call x1, Pallas kernels, relayout(): pl.pallas_call(relayout_kernel, out_shape=(shape((groups, SUB, LANES, LAN...  7.15 us
    all_to_all x1, starting transfers between devices, per_device(): lax.all_to_all(outgoing, ('atm', 'ocn'), split_axis=0, concat_axis=0, til...  7.1 us
    all_to_all x1, starting transfers between devices, per_device(): lax.all_to_all(answer, ('atm', 'ocn'), split_axis=0, concat_axis=0, tiled...  7.09 us
    ppermute x1, waiting for transfers between devices, per_device(): north = lax.ppermute(last, 'atm', forward)  5.44 us
    ppermute x1, starting transfers between devices, per_device(): from_west = lax.ppermute(to_east, 'ocn', forward)  5.05 us
    pallas_call x1, Pallas kernels, down(): pl.pallas_call(down_kernel, out_shape=(shape(((levels - 1) * count, LANES...  4.7 us
  transfers between devices with their start and end apart: 6, of which 1 were waited for; matrix products, arithmetic and copies ran while one was open for 0% of the time, Pallas kernels for 17%

commit v1 on v0

v1 whole, which is shorter than its diff:
```python
import functools

import jax
import jax.numpy as jnp
from jax import lax
from jax.experimental import pallas as pl
from jax.experimental.pallas import tpu as pltpu
from jax.sharding import PartitionSpec as P

NSUB = 4
SUB = 8
LANES = 128
GRANT = 52
F32 = jnp.float32
BF16 = jnp.bfloat16
VMEM = pl.BlockSpec(memory_space=pltpu.VMEM)
ANY = pl.BlockSpec(memory_space=pl.ANY)


def shape(dims, kind=F32):
    return jax.ShapeDtypeStruct(dims, kind)


def round_up(value, unit):
    return -(-value // unit) * unit


def params(mib):
    return pltpu.CompilerParams(vmem_limit_bytes=mib * 2**20)


def cost(flops, moved):
    return pl.CostEstimate(flops=int(flops), bytes_accessed=int(moved), transcendentals=0)


def row_pack_kernel(tracer, speed, first, last, head, tail, sem):
    tracer_count, rows, _ = tracer.shape
    speed_count = speed.shape[0]
    total = tracer_count + speed_count
    copies = []
    for place, (start, into) in enumerate(((0, head), (rows - SUB, tail))):
        copies.append(
            pltpu.make_async_copy(
                tracer.at[:, pl.ds(start, SUB), :], into.at[pl.ds(0, tracer_count)], sem.at[place, 0]
            )
        )
        copies.append(
            pltpu.make_async_copy(
                speed.at[:, pl.ds(start, SUB), :],
                into.at[pl.ds(tracer_count, speed_count)],
                sem.at[place, 1],
            )
        )
    for copy in copies:
        copy.start()
    spare = head.shape[0] - total
    for into in (head, tail):
        into[pl.ds(total, spare)] = jnp.zeros((spare, SUB, LANES), F32)
    for copy in copies:
        copy.wait()
    for into, out, shift in ((head, first, 0), (tail, last, SUB - NSUB)):
        flat = into.reshape(into.shape[0] * SUB, LANES)
        for row in range(NSUB):
            for part in range(0, into.shape[0], 16):
                out[row, pl.ds(part, 16), :] = flat[
                    pl.ds(part * SUB + shift + row, 16, stride=SUB), :
                ].astype(BF16)


def row_pack(tracer, speed):
    total = round_up(tracer.shape[0] + speed.shape[0], 16)
    return pl.pallas_call(
        row_pack_kernel,
        out_shape=(shape((NSUB, total, LANES), BF16),) * 2,
        in_specs=[ANY, ANY],
        out_specs=(VMEM, VMEM),
        scratch_shapes=[
            pltpu.VMEM((total, SUB, LANES), F32),
            pltpu.VMEM((total, SUB, LANES), F32),
            pltpu.SemaphoreType.DMA((2, 2)),
        ],
        compiler_params=params(GRANT),
        cost_estimate=cost(1e6, 4e6),
        name="row_pack",
    )(tracer, speed)


def down_kernel(
    profile, diffusion, slots, blocks, weight, after, coef_c, coef_g, recip, out,
    given, mixing, slot, block, held, prof, diff, made_c, made_g, made_r, placed, total, sent, sem, level_sem,
):
    fields, levels, columns = profile.shape
    count = columns // LANES
    width = fields + 1
    owners = out.shape[0]
    cap = out.shape[1] // width
    rows = cap * width
    lows = range(0, levels, SUB)

    def part(index):
        low = index * SUB
        deep = min(SUB, levels - low)
        return low, deep, min(SUB, levels - 1 - low)

    loads = []
    for index, low in enumerate(lows):
        low, deep, deep_k = part(index)
        pair = [
            pltpu.make_async_copy(
                diffusion.at[pl.ds(low, deep_k)], mixing.at[pl.ds(low, deep_k)], level_sem.at[index, 0]
            ),
            pltpu.make_async_copy(
                profile.at[:, pl.ds(low, deep), :], given.at[:, pl.ds(low, deep), :], level_sem.at[index, 1]
            ),
        ]
        for copy in pair:
            copy.start()
        loads.append(pair)
    others = [
        pltpu.make_async_copy(weight, held, sem.at[0]),
        pltpu.make_async_copy(slots, slot, sem.at[1]),
        pltpu.make_async_copy(blocks, block, sem.at[2]),
    ]
    for copy in others:
        copy.start()
    placed[...] = jnp.zeros(placed.shape, F32)
    total[...] = jnp.zeros(total.shape, F32)
    below = None
    for index, _ in enumerate(lows):
        low, deep, deep_k = part(index)
        for copy in loads[index]:
            copy.wait()
        for place in range(count):
            across = pl.ds(place * LANES, LANES)
            diff[pl.ds(low * count + place, deep_k, stride=count), :] = mixing[pl.ds(low, deep_k), across]
            for field in range(fields):
                prof[field, pl.ds(low * count + place, deep, stride=count), :] = given[
                    field, pl.ds(low, deep), across
                ]
        for level in range(low, low + deep):
            here = pl.ds(level * count, count)
            rhs = [prof[field, here, :] for field in range(fields)]
            bottom = jnp.full((count, LANES), 1.0, F32)
            if level < levels - 1:
                above = diff[here, :]
                bottom = bottom + above
            if level > 0:
                bottom = bottom + below * (1.0 + c_now)
                rhs = [rhs[field] + below * g_now[field] for field in range(fields)]
            inverse = 1.0 / bottom
            g_now = [value * inverse for value in rhs]
            for field in range(fields):
                made_g[field, here, :] = g_now[field]
            if level < levels - 1:
                c_now = -above * inverse
                made_c[here, :] = c_now
                below = above
    made_r[...] = inverse
    results_out = [
        pltpu.make_async_copy(made_c, coef_c, sem.at[3]),
        pltpu.make_async_copy(made_g, coef_g, sem.at[4]),
        pltpu.make_async_copy(made_r, recip, sem.at[5]),
    ]
    for copy in results_out:
        copy.start()
    for number in range(cap):
        for field, value in enumerate(g_now + [inverse]):
            placed[number, pl.ds(number * width + field, count, stride=rows), :] = value
    for copy in others:
        copy.wait()
    step = 8

    def body(group, _):
        results = []
        for inner in range(step):
            at = group * step + inner
            start = pl.multiple_of(block[0, at] * rows, rows)
            left = placed[slot[0, at] % cap, pl.ds(start, rows), :].astype(BF16)
            results.append(
                lax.dot_general(
                    left, held[at], (((1,), (1,)), ((), ())), preferred_element_type=F32
                )
            )
        for inner in range(step):
            owner = slot[0, group * step + inner] // cap
            total[owner] = total[owner] + results[inner]
        return 0

    lax.fori_loop(0, held.shape[0] // step, body, 0)
    for owner in range(owners):
        sent[owner] = total[owner].astype(BF16)
    final = pltpu.make_async_copy(sent, out, sem.at[6])
    final.start()
    for copy in results_out:
        copy.wait()
    final.wait()


def down(profile, diffusion, slots, blocks, weight, after, owners, cap):
    fields, levels, columns = profile.shape
    count = columns // LANES
    rows = cap * (fields + 1)
    padded = round_up(levels, SUB)
    return pl.pallas_call(
        down_kernel,
        out_shape=(
            shape(((levels - 1) * count, LANES)),
            shape((fields, levels * count, LANES)),
            shape((count, LANES)),
            shape((owners, rows, LANES), BF16),
        ),
        in_specs=[ANY] * 5 + [ANY],
        out_specs=(ANY,) * 4,
        scratch_shapes=[
            pltpu.VMEM((fields, padded, columns), F32),
            pltpu.VMEM((padded, columns), F32),
            pltpu.SMEM(slots.shape, jnp.int32),
            pltpu.SMEM(blocks.shape, jnp.int32),
            pltpu.VMEM(weight.shape, BF16),
            pltpu.VMEM((fields, levels * count, LANES), F32),
            pltpu.VMEM(((levels - 1) * count, LANES), F32),
            pltpu.VMEM(((levels - 1) * count, LANES), F32),
            pltpu.VMEM((fields, levels * count, LANES), F32),
            pltpu.VMEM((count, LANES), F32),
            pltpu.VMEM((cap, count * rows, LANES), F32),
            pltpu.VMEM((owners, rows, LANES), F32),
            pltpu.VMEM((owners, rows, LANES), BF16),
            pltpu.SemaphoreType.DMA((7,)),
            pltpu.SemaphoreType.DMA((padded // SUB, 2)),
        ],
        compiler_params=params(GRANT),
        cost_estimate=cost(1e7, 6e6),
        name="down_sweep",
    )(profile, diffusion, slots, blocks, weight, after)


def flux_kernel(
    arrived_at, recv_at, coef_at, kind_at, ice_at, tracer, after, later, fluxes_at, answer_at,
    arrived, recv, coef, kind, ice, surface, fluxes, answer, sem, *, atm, ocn
):
    loads = [
        pltpu.make_async_copy(source, into, sem.at[place])
        for place, (source, into) in enumerate(
            (
                (recv_at, recv),
                (arrived_at, arrived),
                (coef_at, coef),
                (kind_at, kind),
                (ice_at, ice),
                (tracer.at[:, pl.ds(0, 1)], surface),
            )
        )
    ]
    for copy in loads:
        copy.start()
    fields, rows, _ = ice.shape
    width = fields + 1
    slot_total = recv.shape[1]
    chunk = answer.shape[1]
    back = arrived.shape[0] // answer.shape[0]
    spread = (
        lax.broadcasted_iota(jnp.int32, (slot_total, slot_total * width), 1) // width
        == lax.broadcasted_iota(jnp.int32, (slot_total, slot_total * width), 0)
    ).astype(F32).astype(BF16)
    loads[0].wait()
    row_of = jnp.broadcast_to(recv[...], (SUB, slot_total)).astype(F32).astype(BF16)
    row_of = jnp.dot(row_of, spread, preferred_element_type=F32)[0:1]
    lane = lax.broadcasted_iota(jnp.int32, (1, slot_total * width), 1)
    key = row_of.astype(jnp.int32) * width + lane % width
    line = lax.broadcasted_iota(jnp.int32, (width * rows, 1), 0)
    chosen = ((line % rows) * width + line // rows == key).astype(F32)
    for copy in loads[1:]:
        copy.wait()
    summed = jnp.dot(chosen.astype(BF16), arrived[...], preferred_element_type=F32)
    hold = jnp.where(kind[...] != 0, coef[...], 0.0)
    over = 1.0 + hold * summed[fields * rows : (fields + 1) * rows]
    rounded = []
    for field in range(fields):
        top = jnp.where(kind[...] == 2, ice[field], surface[field, 0])
        value = hold * (top - summed[field * rows : (field + 1) * rows]) / over
        fluxes[field] = value
        rounded.append(value.astype(BF16).astype(F32))
    stacked = jnp.concatenate(rounded + [jnp.zeros((rows, LANES), F32)], axis=0).astype(BF16)
    turned = chosen.T.astype(BF16)
    returned = jnp.dot(turned, stacked, preferred_element_type=F32)
    answer[:, pl.ds(0, back), :] = returned.astype(BF16).reshape(answer.shape[0], back, LANES)
    answer[:, pl.ds(back, chunk - back), :] = jnp.zeros((answer.shape[0], chunk - back, LANES), BF16)

    source = lax.broadcasted_iota(jnp.int32, (LANES, 3 * LANES), 0)
    target = lax.broadcasted_iota(jnp.int32, (LANES, 3 * LANES), 1)
    own = source + NSUB
    south = source + rows + NSUB
    north = source - (rows - NSUB)
    pos = jnp.where(target < LANES, own, jnp.where(target < 2 * LANES, south, north))
    fits = (
        ((target < LANES) & (source < rows))
        | ((target >= LANES) & (target < 2 * LANES) & (source < NSUB))
        | ((target >= 2 * LANES) & (source >= rows - NSUB) & (source < rows))
    )
    place = (fits & ((pos % SUB) * SUB + pos // SUB == target % LANES)).astype(F32).astype(BF16)
    sides = []
    for field in range(fields):
        tall = jnp.concatenate([rounded[field], jnp.zeros((LANES - rows, LANES), F32)], axis=0)
        sides.append(jnp.dot(tall.T.astype(BF16), place, preferred_element_type=F32))
    blank = jnp.zeros((chunk - back - fields * NSUB, LANES), F32)
    i = lax.axis_index("atm")
    j = lax.axis_index("ocn")
    for di in (-1, 0, 1):
        for dj in (-1, 0, 1):
            if di == 0 and dj == 0:
                continue
            pieces = []
            for field in range(fields):
                if dj == 0:
                    low = 0 if di < 0 else rows - NSUB
                    pieces.append(rounded[field][low : low + NSUB])
                else:
                    low = 0 if dj < 0 else LANES - NSUB
                    part = {0: 0, -1: 1, 1: 2}[di] * LANES
                    pieces.append(sides[field][low : low + NSUB, part : part + LANES])
            tile = jnp.concatenate(pieces + [blank], axis=0).astype(BF16)

            @pl.when((i + di >= 0) & (i + di < atm) & (j + dj >= 0) & (j + dj < ocn))
            def _():
                answer[(i + di) * ocn + j + dj, pl.ds(back, chunk - back), :] = tile

    stores = [
        pltpu.make_async_copy(answer, answer_at, sem.at[6]),
        pltpu.make_async_copy(fluxes, fluxes_at, sem.at[7]),
    ]
    for copy in stores:
        copy.start()
    for copy in stores:
        copy.wait()


def flux_step(arrived, recv, coef, kind, ice, tracer, after, later, owners, atm, ocn):
    fields, rows, _ = ice.shape
    back = arrived.shape[0] // owners
    chunk = back + round_up(fields * NSUB, 16)
    return pl.pallas_call(
        functools.partial(flux_kernel, atm=atm, ocn=ocn),
        out_shape=(shape(ice.shape), shape((owners, chunk, LANES), BF16)),
        in_specs=[ANY] * 8,
        out_specs=(ANY, ANY),
        scratch_shapes=[
            pltpu.VMEM(arrived.shape, BF16),
            pltpu.VMEM(recv.shape, jnp.int32),
            pltpu.VMEM(coef.shape, F32),
            pltpu.VMEM(kind.shape, jnp.int32),
            pltpu.VMEM(ice.shape, F32),
            pltpu.VMEM((fields, 1, rows, LANES), F32),
            pltpu.VMEM(ice.shape, F32),
            pltpu.VMEM((owners, chunk, LANES), BF16),
            pltpu.SemaphoreType.DMA((8,)),
        ],
        compiler_params=params(GRANT),
        cost_estimate=cost(1e7, 1e6),
        name="flux_step",
    )(arrived, recv, coef, kind, ice, tracer, after, later)


def spot(column, across):
    return column % across * SUB + column // across


def relayout_kernel(
    tracer, speed, north_at, south_at, out, west, east, north, south, raw, tall, plain, done, sem, fetched, stored
):
    halos = [
        pltpu.make_async_copy(north_at, north, sem.at[0]),
        pltpu.make_async_copy(south_at, south, sem.at[1]),
    ]
    for copy in halos:
        copy.start()
    tracer_count, rows, _ = tracer.shape
    total = tracer_count + speed.shape[0]
    groups = out.shape[0]
    size = total // groups
    high = rows + 2 * NSUB
    wide = out.shape[2]
    across = wide // SUB

    def fetch(group):
        here = raw.at[pl.ds(group * size, size)]
        return here, fetched.at[group]

    for group in range(groups):
        into, sem = fetch(group)
        if (group + 1) * size <= tracer_count:
            source = tracer.at[pl.ds(group * size, size)]
        else:
            source = speed.at[pl.ds(group * size - tracer_count, size)]
        pltpu.make_async_copy(source, into, sem).start()
    padded_total = north.shape[1]
    tall[pl.ds(total * high, (padded_total - total) * high), :] = jnp.zeros(
        ((padded_total - total) * high, LANES), F32
    )
    for copy in halos:
        copy.wait()
    for row in range(NSUB):
        for part in range(0, padded_total, 16):
            for halo, start in ((north, 0), (south, rows + NSUB)):
                tall[pl.ds(part * high + start + row, 16, stride=high), :] = halo[
                    row, pl.ds(part, 16), :
                ].astype(F32)

    def body(group, _):
        into, sem = fetch(group)
        pltpu.make_async_copy(into, into, sem).wait()
        for level in range(size):
            tall[pl.ds(pl.multiple_of(group * size * high, SUB) + level * high + NSUB, rows), :] = raw[
                group * size + level
            ]
        for fine in range(SUB):
            stack = tall[pl.ds(group * size * high + fine, LANES, stride=SUB), :]
            plain[fine, pl.ds(SUB, LANES), :] = stack.T
            for step in range(across):
                done[group, fine, pl.ds(step * SUB, SUB), :] = plain[
                    fine, pl.ds(SUB - NSUB + step, SUB, stride=across), :
                ]
        pltpu.make_async_copy(done.at[group], out.at[group], stored.at[group]).start()
        return 0

    lax.fori_loop(0, groups, body, 0)
    slabs = groups * SUB
    flat = done.reshape(slabs * wide, LANES)
    for message, start in ((west, NSUB), (east, wide - 2 * NSUB)):
        for column in range(NSUB):
            at = spot(start + column, across)
            for part in range(0, message.shape[1], 16):
                pieces = []
                for low in (part, part + SUB):
                    if low < slabs:
                        pieces.append(flat[pl.ds(low * wide + at, SUB, stride=wide), :])
                    else:
                        pieces.append(jnp.zeros((SUB, LANES), F32))
                message[column, pl.ds(part, 16), :] = jnp.concatenate(pieces, axis=0).astype(BF16)
    for group in range(groups):
        pltpu.make_async_copy(done.at[group], out.at[group], stored.at[group]).wait()


def relayout(tracer, speed, north, south, size):
    rows = tracer.shape[1]
    total = tracer.shape[0] + speed.shape[0]
    groups = total // size
    slabs = round_up(groups * SUB, 16)
    wide = LANES + 2 * NSUB
    return pl.pallas_call(
        relayout_kernel,
        out_shape=(
            shape((groups, SUB, wide, LANES)),
            shape((NSUB, slabs, LANES), BF16),
            shape((NSUB, slabs, LANES), BF16),
        ),
        in_specs=[ANY, ANY, ANY, ANY],
        out_specs=(ANY, VMEM, VMEM),
        scratch_shapes=[
            pltpu.VMEM(north.shape, BF16),
            pltpu.VMEM(south.shape, BF16),
            pltpu.VMEM((total, rows, LANES), F32),
            pltpu.VMEM((north.shape[1] * (rows + 2 * NSUB), LANES), F32),
            pltpu.VMEM((SUB, LANES + 2 * SUB, LANES), F32),
            pltpu.VMEM((groups, SUB, wide, LANES), F32),
            pltpu.SemaphoreType.DMA((2,)),
            pltpu.SemaphoreType.DMA((groups,)),
            pltpu.SemaphoreType.DMA((groups,)),
        ],
        compiler_params=params(GRANT),
        cost_estimate=cost(1e7, 1.4e7),
        name="relayout",
    )(tracer, speed, north, south)


def up_part(
    answer, out, slot, block, held, made_c, made_g, made_r, sums, solved, final, first, weights, later, out_sem
):
    fields, levels, columns = out.shape
    count = columns // LANES
    width = fields + 1
    rows = sums.shape[1]
    cap = rows // width
    parts = len(weights)
    share = held.shape[0] // parts
    sums[...] = jnp.zeros(sums.shape, F32)
    slot_row = lax.broadcasted_iota(jnp.int32, (rows, LANES), 0) // width
    step = 8

    def body(group, _):
        results = []
        for inner in range(step):
            at = group * step + inner
            left = answer[slot[0, at] // cap, pl.ds(0, rows), :]
            results.append(jnp.dot(left, held[at], preferred_element_type=F32))
        for inner in range(step):
            at = group * step + inner
            kept = jnp.where(slot_row == slot[0, at] % cap, results[inner], 0.0)
            sums[block[0, at]] = sums[block[0, at]] + kept
        return 0

    for copy in first:
        copy.wait()
    for part in range(parts):
        weights[part].wait()
        lax.fori_loop(part * share // step, (part + 1) * share // step, body, 0)
    for copy in later:
        copy.wait()
    flat = sums.reshape(count * rows, LANES)
    now = []
    last = pl.ds((levels - 1) * count, count)
    for field in range(fields):
        flux = flat[pl.ds(field, count, stride=rows), :]
        for number in range(1, cap):
            flux = flux + flat[pl.ds(number * width + field, count, stride=rows), :]
        now.append(made_g[field, last, :] + made_r[...] * flux)
        solved[field, last, :] = now[field]
    copies = []
    for low in reversed(range(0, levels, SUB)):
        deep = min(SUB, levels - low)
        for level in range(min(low + deep, levels - 1) - 1, low - 1, -1):
            here = pl.ds(level * count, count)
            for field in range(fields):
                now[field] = made_g[field, here, :] - made_c[here, :] * now[field]
                solved[field, here, :] = now[field]
        for field in range(fields):
            for place in range(count):
                final[field, pl.ds(low, deep), pl.ds(place * LANES, LANES)] = solved[
                    field, pl.ds(low * count + place, deep, stride=count), :
                ]
        copies.append(
            pltpu.make_async_copy(
                final.at[:, pl.ds(low, deep), :], out.at[:, pl.ds(low, deep), :], out_sem.at[low // SUB]
            )
        )
        copies[-1].start()
    return copies


class Transport:
    def __init__(self, laid, from_west_at, from_east_at, out, scratch, fields, first, count):
        self.laid, self.out, self.fields, self.first, self.count = laid, out, fields, first, count
        (
            self.from_west, self.from_east, self.here, self.there, self.speed, self.along, self.cross,
            self.halo, self.plain, self.high, self.raw, self.sem, self.fetched, self.stored,
        ) = scratch
        self.per = laid.shape[0] // (fields + 2)
        self.size = out.shape[0] // (fields * self.per)
        self.rows = out.shape[1]
        self.wide = laid.shape[2]
        self.across = self.wide // SUB
        self.smalls = [
            pltpu.make_async_copy(from_west_at, self.from_west, self.sem.at[0]),
            pltpu.make_async_copy(from_east_at, self.from_east, self.sem.at[1]),
        ]

    @staticmethod
    def scratch(laid_shape, message_shape, out_rows, size, fields, count):
        groups, _, wide, _ = laid_shape
        return [
            pltpu.VMEM(message_shape, BF16),
            pltpu.VMEM(message_shape, BF16),
            pltpu.VMEM((fields * count, SUB, wide, LANES), F32),
            pltpu.VMEM((fields, SUB, wide, LANES), F32),
            pltpu.VMEM((2 * count, SUB, wide, LANES), F32),
            pltpu.VMEM((SUB + 1, wide, LANES), F32),
            pltpu.VMEM((SUB, wide, LANES), F32),
            pltpu.VMEM((2,) + message_shape, F32),
            pltpu.VMEM((SUB, LANES + 2 * SUB, LANES), F32),
            pltpu.VMEM((fields, SUB * LANES, LANES), F32),
            pltpu.VMEM((fields * count * size, out_rows, LANES), F32),
            pltpu.SemaphoreType.DMA((2,)),
            pltpu.SemaphoreType.DMA((fields + 2, count)),
            pltpu.SemaphoreType.DMA((fields, count)),
        ]

    def fetch(self, array, turn):
        group = array * self.per + self.first + turn
        if array < self.fields:
            into = self.here.at[array * self.count + turn]
        else:
            into = self.speed.at[(array - self.fields) * self.count + turn]
        return pltpu.make_async_copy(self.laid.at[group], into, self.fetched.at[array, turn])

    def store(self, field, turn):
        start = (field * self.per + self.first + turn) * self.size
        return pltpu.make_async_copy(
            self.raw.at[pl.ds((field * self.count + turn) * self.size, self.size)],
            self.out.at[pl.ds(start, self.size)],
            self.stored.at[field, turn],
        )

    def start(self, turn):
        for array in range(self.fields + 2):
            self.fetch(array, turn).start()
        if turn == 0:
            for copy in self.smalls:
                copy.start()

    def messages(self):
        for copy in self.smalls:
            copy.wait()
        for column in range(NSUB):
            self.halo[0, column] = self.from_west[column].astype(F32)
            self.halo[1, column] = self.from_east[column].astype(F32)

    def ready(self, turn):
        wide = self.wide
        for array in range(self.fields + 2):
            self.fetch(array, turn).wait()
            if array < self.fields:
                ref, at = self.here, array * self.count + turn
            else:
                ref, at = self.speed, (array - self.fields) * self.count + turn
            group = array * self.per + self.first + turn
            flat = ref.reshape(ref.shape[0] * SUB * wide, LANES)
            for side in range(2):
                for column in range(NSUB):
                    to = spot(column if side == 0 else wide - NSUB + column, self.across)
                    flat[pl.ds(at * (SUB * wide) + to, SUB, stride=wide), :] = self.halo[
                        side, column, pl.ds(group * SUB, SUB), :
                    ]

    def force(self, neighbour, fluxes, thin):
        fields, rows, across, plain = self.fields, self.rows, self.across, self.plain
        thin[...] = jnp.zeros(thin.shape, F32)
        up_rows = neighbour(-1, 0)
        down_rows = neighbour(1, 0)
        for field in range(fields):
            thin[field, pl.ds(0, NSUB), :] = up_rows[field * NSUB : (field + 1) * NSUB]
            thin[field, pl.ds(NSUB, rows), :] = fluxes[field]
            thin[field, pl.ds(NSUB + rows, NSUB), :] = down_rows[field * NSUB : (field + 1) * NSUB]
        lane = lax.broadcasted_iota(jnp.int32, (16, LANES), 1)
        sides = [sum(neighbour(di, dj) for di in (-1, 0, 1)) for dj in (-1, 1)]
        for fine in range(SUB):
            moved = []
            for side in sides:
                turned = side if fine == 0 else pltpu.roll(side, LANES - SUB * fine, 1)
                moved.append(jnp.where(lane < SUB, turned, 0.0))
            for field in range(fields):
                few = thin[field, pl.ds(fine, SUB, stride=SUB), :]
                stack = jnp.concatenate([few, jnp.zeros((LANES - SUB, LANES), F32)], axis=0)
                plain[field, pl.ds(SUB, LANES), :] = stack.T
                plain[field, pl.ds(SUB - NSUB, NSUB), :] = moved[0][field * NSUB : (field + 1) * NSUB]
                plain[field, pl.ds(SUB + LANES, NSUB), :] = moved[1][field * NSUB : (field + 1) * NSUB]
                for step in range(across):
                    at = (field * self.count, fine, pl.ds(step * SUB, SUB))
                    self.here[at] = (
                        self.here[at] - plain[field, pl.ds(SUB - NSUB + step, SUB, stride=across), :]
                    )

    def faces(self, turn):
        speed, along, cross, across = self.speed, self.along, self.cross, self.across
        for step in range(across):
            at = pl.ds(step * SUB, SUB)
            after = pl.ds(step * SUB + SUB, SUB) if step < across - 1 else pl.ds(1, SUB)
            rows_here = [speed[turn, fine, at, :] for fine in range(SUB)]
            rows_here.append(pltpu.roll(rows_here[0], LANES - 1, 1))
            for fine in range(SUB):
                face = 0.5 * (rows_here[fine] + rows_here[fine + 1])
                along[fine + 1, at, :] = face
                if fine == SUB - 1:
                    along[0, at, :] = pltpu.roll(face, 1, 1)
                lead = (self.count + turn, fine)
                cross[fine, at, :] = 0.5 * (speed[lead + (at,)] + speed[lead + (after,)])

    def update(self, src, src_at, dst, dst_at):
        along, cross, fields, across, wide = self.along, self.cross, self.fields, self.across, self.wide
        last = pl.ds(wide - SUB - 1, SUB)
        first = pl.ds(0, SUB)
        now = [[src[src_at[f], fine, first, :] for fine in range(SUB)] for f in range(fields)]
        carried = [[None] * SUB for _ in range(fields)]
        for fine in range(SUB):
            face = cross[fine, last, :]
            for f in range(fields):
                before = src[src_at[f], fine, last, :]
                carried[f][fine] = face * jnp.where(face > 0.0, before, now[f][fine])
        for step in range(across):
            at = pl.ds(step * SUB, SUB)
            after = pl.ds(step * SUB + SUB, SUB) if step < across - 1 else pl.ds(1, SUB)
            flow = []
            wrap = []
            face = along[0, at, :]
            for f in range(fields):
                above = pltpu.roll(now[f][SUB - 1], 1, 1)
                wrap.append(pltpu.roll(now[f][0], LANES - 1, 1))
                flow.append(face * jnp.where(face > 0.0, above, now[f][0]))
            for fine in range(SUB):
                down_face = along[fine + 1, at, :]
                side_face = cross[fine, at, :]
                down_pick = down_face > 0.0
                side_pick = side_face > 0.0
                for f in range(fields):
                    value = now[f][fine]
                    lower = now[f][fine + 1] if fine < SUB - 1 else wrap[f]
                    right = src[src_at[f], fine, after, :]
                    down_flow = down_face * jnp.where(down_pick, value, lower)
                    side_flow = side_face * jnp.where(side_pick, value, right)
                    dst[dst_at[f], fine, at, :] = (
                        value + (flow[f] - down_flow) + (carried[f][fine] - side_flow)
                    )
                    flow[f] = down_flow
                    carried[f][fine] = side_flow
                    now[f][fine] = right

    def run(self, turn):
        fields, across, plain = self.fields, self.across, self.plain
        tall = self.rows + 2 * NSUB
        self.faces(turn)
        mine = [field * self.count + turn for field in range(fields)]
        spare = list(range(fields))

        def pair(_, carry):
            self.update(self.here, mine, self.there, spare)
            self.update(self.there, spare, self.here, mine)
            return carry

        lax.fori_loop(0, NSUB // 2, pair, 0)
        for field in range(fields):
            lead = field * self.count + turn
            for fine in range(SUB):
                for step in range(across):
                    plain[fine, pl.ds(SUB - NSUB + step, SUB, stride=across), :] = self.here[
                        lead, fine, pl.ds(step * SUB, SUB), :
                    ]
                self.high[field, pl.ds(fine, LANES, stride=SUB), :] = plain[fine, pl.ds(SUB, LANES), :].T
            base = lead * self.size
            for level in range(self.size):
                self.raw[base + level] = self.high[field, pl.ds(level * tall + NSUB, self.rows), :]
            self.store(field, turn).start()

    def finish(self):
        for field in range(self.fields):
            for turn in range(self.count):
                self.store(field, turn).wait()


def up_kernel(
    answered_at, slots, blocks, weight, coef_c, coef_g, recip,
    out, answered, slot, block, held, made_c, made_g, made_r, sums, solved, final, sem, out_sem, *, parts
):
    share = held.shape[0] // parts
    first = [
        pltpu.make_async_copy(answered_at, answered, sem.at[0]),
        pltpu.make_async_copy(slots, slot, sem.at[1]),
        pltpu.make_async_copy(blocks, block, sem.at[2]),
    ]
    weights = [
        pltpu.make_async_copy(
            weight.at[pl.ds(part * share, share)], held.at[pl.ds(part * share, share)], sem.at[6 + part]
        )
        for part in range(parts)
    ]
    later = [
        pltpu.make_async_copy(recip, made_r, sem.at[5]),
        pltpu.make_async_copy(coef_g, made_g, sem.at[4]),
        pltpu.make_async_copy(coef_c, made_c, sem.at[3]),
    ]
    for copy in first + weights + later:
        copy.start()
    leaving = up_part(
        answered, out, slot, block, held, made_c, made_g, made_r, sums, solved, final,
        first, weights, later, out_sem,
    )
    for copy in leaving:
        copy.wait()


def up(answered, slots, blocks, weight, coef_c, coef_g, recip, levels, cap):
    fields = coef_g.shape[0]
    count = recip.shape[0]
    rows = cap * (fields + 1)
    padded = round_up(levels, SUB)
    parts = 4
    return pl.pallas_call(
        functools.partial(up_kernel, parts=parts),
        out_shape=shape((fields, levels, count * LANES)),
        in_specs=[ANY] * 7,
        out_specs=ANY,
        scratch_shapes=[
            pltpu.VMEM(answered.shape, BF16),
            pltpu.SMEM(slots.shape, jnp.int32),
            pltpu.SMEM(blocks.shape, jnp.int32),
            pltpu.VMEM(weight.shape, BF16),
            pltpu.VMEM(coef_c.shape, F32),
            pltpu.VMEM(coef_g.shape, F32),
            pltpu.VMEM(recip.shape, F32),
            pltpu.VMEM((count, rows, LANES), F32),
            pltpu.VMEM((fields, levels * count, LANES), F32),
            pltpu.VMEM((fields, padded, count * LANES), F32),
            pltpu.SemaphoreType.DMA((6 + parts,)),
            pltpu.SemaphoreType.DMA((padded // SUB,)),
        ],
        compiler_params=params(GRANT),
        cost_estimate=cost(1e7, 6e6),
        name="up_sweep",
    )(answered, slots, blocks, weight, coef_c, coef_g, recip)


def advect_kernel(
    laid, from_west, from_east, fluxes_at, answered_at, out, answered, fluxes, thin, sem, *scratch,
    fields, atm, ocn
):
    per = laid.shape[0] // (fields + 2)
    ocean = Transport(laid, from_west, from_east, out, scratch, fields, 0, per)
    smalls = [
        pltpu.make_async_copy(answered_at, answered, sem.at[0]),
        pltpu.make_async_copy(fluxes_at, fluxes, sem.at[1]),
    ]
    ocean.start(0)
    for copy in smalls:
        copy.start()
    i = lax.axis_index("atm")
    j = lax.axis_index("ocn")
    back = answered.shape[1] - round_up(fields * NSUB, 16)

    def neighbour(di, dj):
        inside = (i + di >= 0) & (i + di < atm) & (j + dj >= 0) & (j + dj < ocn)
        index = jnp.where(inside, (i + di) * ocn + j + dj, 0)
        value = answered[index, pl.ds(back, answered.shape[1] - back), :].astype(F32)
        return jnp.where(inside, value, 0.0)

    ocean.messages()
    ocean.ready(0)
    for turn in range(1, per):
        ocean.start(turn)
    for copy in smalls:
        copy.wait()
    ocean.force(neighbour, fluxes, thin)

    def body(turn, carry):
        ocean.run(turn)
        for later in range(1, per):
            pl.when(turn == later - 1)(functools.partial(ocean.ready, later))
        return carry

    lax.fori_loop(0, per, body, 0)
    ocean.finish()


def advect(laid, from_west, from_east, fluxes, answered, rows, size, atm, ocn):
    fields = fluxes.shape[0]
    per = laid.shape[0] // (fields + 2)
    return pl.pallas_call(
        functools.partial(advect_kernel, fields=fields, atm=atm, ocn=ocn),
        out_shape=shape((fields * per * size, rows, LANES)),
        in_specs=[ANY] * 5,
        out_specs=ANY,
        scratch_shapes=[
            pltpu.VMEM(answered.shape, BF16),
            pltpu.VMEM(fluxes.shape, F32),
            pltpu.VMEM((fields, SUB * SUB, LANES), F32),
            pltpu.SemaphoreType.DMA((2,)),
        ]
        + Transport.scratch(laid.shape, from_west.shape, rows, size, fields, per),
        compiler_params=params(GRANT),
        cost_estimate=cost(5e7, 1.2e7),
        name="advect",
    )(laid, from_west, from_east, fluxes, answered)


def per_device(
    atm_state,
    diffusivity,
    send_slot,
    atm_block,
    recv_row,
    remap_weight,
    ocean_tracer,
    ocean_velocity,
    exchange_coef,
    surface_kind,
    ice_surface,
):
    atm, ocn = lax.axis_size("atm"), lax.axis_size("ocn")
    owners = atm * ocn
    fields, levels, _ = atm_state.shape
    cap = recv_row.shape[1] // owners
    depth, rows, columns = ocean_tracer.shape[1:]
    most = LANES // ((rows + 2 * NSUB) // SUB)
    size = max(count for count in range(1, most + 1) if depth % count == 0)
    tracer = ocean_tracer.reshape(-1, rows, columns)
    speed = ocean_velocity.reshape(-1, rows, columns)

    def neighbours(axis):
        count = lax.axis_size(axis)
        up = [(place, place + 1) for place in range(count - 1)]
        return up, [(target, source) for source, target in up]

    forward, backward = neighbours("atm")
    first, last = row_pack(tracer, speed)
    south = lax.ppermute(first, "atm", backward)
    north = lax.ppermute(last, "atm", forward)
    coef_c, coef_g, recip, outgoing = down(
        atm_state, diffusivity, send_slot, atm_block, remap_weight, first, owners, cap
    )
    arrived = lax.all_to_all(outgoing, ("atm", "ocn"), split_axis=0, concat_axis=0, tiled=True)
    fluxes, answer = flux_step(
        arrived.reshape(-1, LANES), recv_row, exchange_coef, surface_kind, ice_surface,
        ocean_tracer, north, south, owners, atm, ocn,
    )
    answered = lax.all_to_all(answer, ("atm", "ocn"), split_axis=0, concat_axis=0, tiled=True)
    laid, to_west, to_east = relayout(tracer, speed, north, south, size)
    forward, backward = neighbours("ocn")
    from_east = lax.ppermute(to_west, "ocn", backward)
    from_west = lax.ppermute(to_east, "ocn", forward)
    atm_new = up(
        answered, send_slot, atm_block, remap_weight, coef_c, coef_g, recip, levels, cap
    )
    ocean_new = advect(laid, from_west, from_east, fluxes, answered, rows, size, atm, ocn)
    return atm_new, ocean_new.reshape(ocean_tracer.shape)


def solution(mesh):
    placed = (
        P(None, None, ("atm", "ocn")),
        P(None, ("atm", "ocn")),
        P(("atm", "ocn"), None),
        P(("atm", "ocn"), None),
        P(("atm", "ocn"), None),
        P(("atm", "ocn"), None, None),
        P(None, None, "atm", "ocn"),
        P(None, None, "atm", "ocn"),
        P("atm", "ocn"),
        P("atm", "ocn"),
        P(None, "atm", "ocn"),
    )
    return jax.shard_map(
        per_device,
        mesh=mesh,
        in_specs=placed,
        out_specs=(P(None, None, ("atm", "ocn")), P(None, None, "atm", "ocn")),
        check_vma=False,
    )
```

time: 83.1 us -> 64.1 us (0.77); the launches traced: 81.6 us -> 63.6 us
  blocking collectives: 0 us -> 15.7 us
  local copies, waits for them, and re-layouts: 13.7 us -> 0.04 us
  starting transfers between devices: 26.5 us -> 14.1 us
  waiting for transfers between devices: 5.46 us -> 0.27 us
  Pallas kernels: 35 us -> 32.7 us
    all_to_all x0 -> x1, blocking collectives: none -> 15.7 us  [per_device(): lax.all_to_all(outgoing, ('atm', 'ocn'), split_axis=0, concat_axis=0, til...]
    unnamed x34 -> x14, local copies, waits for them, and re-layouts: 13.7 us -> 0.04 us
    all_to_all x1 -> x0, starting transfers between devices: 7.1 us -> none  [per_device(): lax.all_to_all(outgoing, ('atm', 'ocn'), split_axis=0, concat_axis=0, til...]
    ppermute x1, waiting for transfers between devices: 5.44 us -> 0.01 us  [per_device(): north = lax.ppermute(last, 'atm', forward)]
    pallas_call x1, Pallas kernels: 16.2 us -> 12.4 us  [advect(): pl.pallas_call(functools.partial(advect_kernel, fields=fields, atm=atm, o...]
    all_to_all x1, starting transfers between devices: 7.09 us -> 3.26 us  [per_device(): lax.all_to_all(answer, ('atm', 'ocn'), split_axis=0, concat_axis=0, tiled...]
    ppermute x1, starting transfers between devices: 5.05 us -> 3.54 us  [per_device(): from_west = lax.ppermute(to_east, 'ocn', forward)]
  transfers between devices with their start and end apart: 6 -> 5, of which waited for: 1 -> 1; matrix products, arithmetic and copies ran while one was open for 0% -> 0% of each run, Pallas kernels for 17% -> 25%
where the time goes in v1:
time: 64.1 us; the launch traced here: 63.6 us
  Pallas kernels  32.7 us (51%)
  blocking collectives  15.7 us (24%)
  starting transfers between devices  14.1 us (22%)
  between operations  0.83 us (1%)
    all_to_all x1, blocking collectives, per_device(): lax.all_to_all(outgoing, ('atm', 'ocn'), split_axis=0, concat_axis=0, til...  15.7 us
    pallas_call x1, Pallas kernels, advect(): pl.pallas_call(functools.partial(advect_kernel, fields=fields, atm=atm, o...  12.4 us
    pallas_call x1, Pallas kernels, relayout(): pl.pallas_call(relayout_kernel, out_shape=(shape((groups, SUB, wide, LANE...  6.17 us
    pallas_call x1, Pallas kernels, down(): pl.pallas_call(down_kernel, out_shape=(shape(((levels - 1) * count, LANES...  5.39 us
    ppermute x1, starting transfers between devices, per_device(): north = lax.ppermute(last, 'atm', forward)  4.1 us
    pallas_call x1, Pallas kernels, up(): pl.pallas_call(functools.partial(up_kernel, parts=parts), out_shape=shape...  4.07 us
    ppermute x1, starting transfers between devices, per_device(): from_west = lax.ppermute(to_east, 'ocn', forward)  3.54 us
    all_to_all x1, starting transfers between devices, per_device(): lax.all_to_all(answer, ('atm', 'ocn'), split_axis=0, concat_axis=0, tiled...  3.26 us
  transfers between devices with their start and end apart: 5, of which 1 were waited for; matrix products, arithmetic and copies ran while one was open for 0% of the time, Pallas kernels for 25%

profile of v1, /device:TPU:1, one launch (start us, length us, event | category | flops | bytes accessed | tf_op | source)
XLA Modules:
  0.0 63.6 jit_solution(17182632358174179974)
XLA Ops:
  0.6 0.0 copy-start
  0.6 0.0 copy-start.4
  0.7 0.0 copy-start.5
  0.7 2.3 %row_pack.1 = (bf16[4,384,128]{2,1,0:T(8,128)(2,1)S(1)}, bf16[4,384,128]{2,1,0:T(8,128)(2,1)S(1)}) custom-call(f32[225,32,128]{2,1,0:T(8,128)} %bitcast.5, f32[150,32,128]{2,1,0:T(8,128)} %bitcast.7), custom_call_target="tpu_custom_call" | custom-call | flops 1000000 | bytes 4000000 | tf_op jit(solution)/shard_map/row_pack/pallas_call | solution.py:72
  2.9 0.0 copy-start.1
  2.9 0.0 copy-start.2
  2.9 0.0 copy-start.3
  3.0 0.0 copy-start.6
  3.0 4.1 %collective-permute-start = (bf16[4,384,128]{2,1,0:T(8,128)(2,1)S(1)}, bf16[4,384,128]{2,1,0:T(8,128)(2,1)S(1)}, u32[]{:S(2)}, u32[]{:S(2)}) collective-permute-start(bf16[4,384,128]{2,1,0:T(8,128)(2,1)S(1)} %get-tuple-element.15), channel_id=1, source_target_pairs={{0,4},{4,8},{8,12},{12,16},{16,20},{20,24},{24,28},{1,5},{5,9},{9,... | collective-permute-start | bytes 1179656 | tf_op jit(solution)/shard_map/ppermute | solution.py:892
  7.1 1.3 %collective-permute-start.1 = (bf16[4,384,128]{2,1,0:T(8,128)(2,1)S(1)}, bf16[4,384,128]{2,1,0:T(8,128)(2,1)S(1)}, u32[]{:S(2)}, u32[]{:S(2)}) collective-permute-start(bf16[4,384,128]{2,1,0:T(8,128)(2,1)S(1)} %get-tuple-element.13.after), channel_id=1, source_target_pairs={{4,0},{8,4},{12,8},{16,12},{20,16},{24,20},{28,24},{5,1},{9,5},{13... | collective-permute-start | bytes 1179656 | tf_op jit(solution)/shard_map/ppermute | solution.py:891
  8.4 0.0 copy-done
  8.4 0.0 copy-done.4
  8.4 0.0 copy-done.5
  8.4 5.4 %down_sweep.1 = (f32[992,128]{1,0:T(8,128)S(1)}, f32[3,1008,128]{2,1,0:T(8,128)}, f32[16,128]{1,0:T(8,128)S(1)}, bf16[32,16,128]{2,1,0:T(8,128)(2,1)S(1)}) custom-call(f32[3,63,2048]{2,1,0:T(8,128)} %profile.1, f32[62,2048]{1,0:T(8,128)S(1)} %copy-done, s32[1,64]{1,0:T(1,128)S(1)} %copy-done.4, s32[1,64]{1,0:T(1,128)S(1)} %copy-done.5, ...), custom_call_target="tpu_custom_call" | custom-call | flops 10000000 | bytes 6000000 | tf_op jit(solution)/shard_map/down_sweep/pallas_call | solution.py:204
  13.8 15.7 %all_to_all.10 = bf16[32,16,128]{2,1,0:T(8,128)(2,1)S(1)} all-to-all(bf16[32,16,128]{2,1,0:T(8,128)(2,1)S(1)} %get-tuple-element.14), channel_id=1, replica_groups=mesh['atm'=8,'ocn'=4] {'atm','ocn'}, dimensions={0} | all-to-all | bytes 262144 | tf_op jit(solution)/shard_map/all_to_all | solution.py:896
  29.5 0.0 collective-permute-done.after.north_at
  29.5 0.0 collective-permute-done.1.later.south_at
  29.5 0.0 copy-done.1
  29.5 0.0 copy-done.2
  29.5 0.0 copy-done.3
  29.5 0.0 copy-done.6
  29.5 2.4 %flux_step.1 = (f32[3,32,128]{2,1,0:T(8,128)S(1)}, bf16[32,32,128]{2,1,0:T(8,128)(2,1)}) custom-call(bf16[512,128]{1,0:T(8,128)(2,1)S(1)} %bitcast.4, s32[1,128]{1,0:T(1,128)S(1)} %copy-done.6, f32[32,128]{1,0:T(8,128)S(1)} %copy-done.2, s32[32,128]{1,0:T(8,128)S(1)} %copy-done.3, f32[3,32,128]{2,1,0:T(8,128)S(1)} %copy-done.1, f32[3,75,32,128]{3,2,1,0:T(8,128)} %tracer.1, ...), custom_call_target="tpu_custom_call" | custom-call | flops 10000000 | bytes 1000000 | tf_op jit(solution)/shard_map/flux_step/pallas_call | solution.py:341
  32.0 3.3 %all-to-all-start.1 = ((bf16[32,32,128]{2,1,0:T(8,128)(2,1)}), bf16[32,32,128]{2,1,0:T(8,128)(2,1)S(1)}, u32[]{:S(2)}, u32[]{:S(2)}) async-start(bf16[32,32,128]{2,1,0:T(8,128)(2,1)} %get-tuple-element.16), calls=%async_computation.1 | async-start | bytes 524288 | tf_op jit(solution)/shard_map/all_to_all | solution.py:901
  35.2 6.2 %relayout.1 = (f32[15,8,136,128]{3,2,1,0:T(8,128)}, bf16[4,128,128]{2,1,0:T(8,128)(2,1)S(1)}, bf16[4,128,128]{2,1,0:T(8,128)(2,1)S(1)}) custom-call(f32[225,32,128]{2,1,0:T(8,128)} %bitcast.6, f32[150,32,128]{2,1,0:T(8,128)} %bitcast.8, bf16[4,384,128]{2,1,0:T(8,128)(2,1)S(1)} %collective-permute-done.after.north_at, ...), custom_call_target="tpu_custom_call" | custom-call | flops 10000000 | bytes 14000000 | tf_op jit(solution)/shard_map/relayout/pallas_call | solution.py:449
  41.4 3.5 %collective-permute-start.2 = (bf16[4,128,128]{2,1,0:T(8,128)(2,1)S(1)}, bf16[4,128,128]{2,1,0:T(8,128)(2,1)S(1)}, u32[]{:S(2)}, u32[]{:S(2)}) collective-permute-start(bf16[4,128,128]{2,1,0:T(8,128)(2,1)S(1)} %get-tuple-element.21), channel_id=1, source_target_pairs={{0,1},{1,2},{2,3},{4,5},{5,6},{6,7},{8,9},{9,10},{10,11},{12,13},{... | collective-permute-start | bytes 393224 | tf_op jit(solution)/shard_map/ppermute | solution.py:905
  45.0 1.9 %collective-permute-start.3 = (bf16[4,128,128]{2,1,0:T(8,128)(2,1)S(1)}, bf16[4,128,128]{2,1,0:T(8,128)(2,1)S(1)}, u32[]{:S(2)}, u32[]{:S(2)}) collective-permute-start(bf16[4,128,128]{2,1,0:T(8,128)(2,1)S(1)} %get-tuple-element.22), channel_id=1, source_target_pairs={{1,0},{2,1},{3,2},{5,4},{6,5},{7,6},{9,8},{10,9},{11,10},{13,12},{... | collective-permute-start | bytes 393224 | tf_op jit(solution)/shard_map/ppermute | solution.py:904
  46.9 0.0 all-to-all-done.1.answered_at
  46.9 4.1 %up_sweep.1 = f32[3,63,2048]{2,1,0:T(8,128)} custom-call(bf16[32,32,128]{2,1,0:T(8,128)(2,1)S(1)} %all-to-all-done.1.answered_at, s32[1,64]{1,0:T(1,128)S(1)} %copy-done.4, s32[1,64]{1,0:T(1,128)S(1)} %copy-done.5, bf16[64,128,128]{2,1,0:T(8,128)(2,1)} %weight.3, f32[992,128]{1,0:T(8,128)S(1)} %get-tuple-element.17.coef_c, ...), custom_call_target="tpu_custom_call" | custom-call | flops 10000000 | bytes 6000000 | tf_op jit(solution)/shard_map/up_sweep/pallas_call | solution.py:774
  51.0 0.0 collective-permute-done.2.from_west
  51.0 0.3 collective-permute-done.3.from_east
  51.3 12.4 %advect.1 = f32[225,32,128]{2,1,0:T(8,128)} custom-call(f32[15,8,136,128]{3,2,1,0:T(8,128)} %get-tuple-element.20.laid, bf16[4,128,128]{2,1,0:T(8,128)(2,1)S(1)} %collective-permute-done.2.from_west, bf16[4,128,128]{2,1,0:T(8,128)(2,1)S(1)} %collective-permute-done.3.from_east, f32[3,32,128]{2,1,0:T(8,128)S(1)} %get-tuple-element.23.fluxes_at, ...), custom_call_target="tpu_custom_call" | custom-call | flops 50000000 | bytes 12000000 | tf_op jit(solution)/shard_map/advect/pallas_call | solution.py:843
Async XLA Ops:
  0.6 7.8 %copy-start = (f32[62,2048]{1,0:T(8,128)S(1)}, f32[62,2048]{1,0:T(8,128)}, u32[]{:S(2)}) copy-start(f32[62,2048]{1,0:T(8,128)} %diffusion.1) | copy-start | bytes 1523716
  0.6 7.8 %copy-start.4 = (s32[1,64]{1,0:T(1,128)S(1)}, s32[1,64]{1,0:T(1,128)}, u32[]{:S(2)}) copy-start(s32[1,64]{1,0:T(1,128)} %slots.3) | copy-start | bytes 772
  0.7 7.8 %copy-start.5 = (s32[1,64]{1,0:T(1,128)S(1)}, s32[1,64]{1,0:T(1,128)}, u32[]{:S(2)}) copy-start(s32[1,64]{1,0:T(1,128)} %blocks.3) | copy-start | bytes 772
  2.9 26.6 %copy-start.1 = (f32[3,32,128]{2,1,0:T(8,128)S(1)}, f32[3,32,128]{2,1,0:T(8,128)}, u32[]{:S(2)}) copy-start(f32[3,32,128]{2,1,0:T(8,128)} %ice_at.1) | copy-start | bytes 147460
  2.9 26.6 %copy-start.2 = (f32[32,128]{1,0:T(8,128)S(1)}, f32[32,128]{1,0:T(8,128)}, u32[]{:S(2)}) copy-start(f32[32,128]{1,0:T(8,128)} %coef_at.1) | copy-start | bytes 49156
  2.9 26.6 %copy-start.3 = (s32[32,128]{1,0:T(8,128)S(1)}, s32[32,128]{1,0:T(8,128)}, u32[]{:S(2)}) copy-start(s32[32,128]{1,0:T(8,128)} %kind_at.1) | copy-start | bytes 49156
  3.0 26.6 %copy-start.6 = (s32[1,128]{1,0:T(1,128)S(1)}, s32[1,128]{1,0:T(1,128)}, u32[]{:S(2)}) copy-start(s32[1,128]{1,0:T(1,128)} %recv_at.1) | copy-start | bytes 1540
  3.0 26.5 %collective-permute-start = (bf16[4,384,128]{2,1,0:T(8,128)(2,1)S(1)}, bf16[4,384,128]{2,1,0:T(8,128)(2,1)S(1)}, u32[]{:S(2)}, u32[]{:S(2)}) collective-permute-start(bf16[4,384,128]{2,1,0:T(8,128)(2,1)S(1)} %get-tuple-element.15), channel_id=1, source_target_pairs={{0,4},{4,8},{8,12},{12,16},{16,20},{20,24},{24,28},{1,5},{5,9},{9,... | collective-permute-start | bytes 1179656 | tf_op jit(solution)/shard_map/ppermute | solution.py:892
  7.1 22.4 %collective-permute-start.1 = (bf16[4,384,128]{2,1,0:T(8,128)(2,1)S(1)}, bf16[4,384,128]{2,1,0:T(8,128)(2,1)S(1)}, u32[]{:S(2)}, u32[]{:S(2)}) collective-permute-start(bf16[4,384,128]{2,1,0:T(8,128)(2,1)S(1)} %get-tuple-element.13.after), channel_id=1, source_target_pairs={{4,0},{8,4},{12,8},{16,12},{20,16},{24,20},{28,24},{5,1},{9,5},{13... | collective-permute-start | bytes 1179656 | tf_op jit(solution)/shard_map/ppermute | solution.py:891
  32.0 14.9 %all-to-all-start.1 = ((bf16[32,32,128]{2,1,0:T(8,128)(2,1)}), bf16[32,32,128]{2,1,0:T(8,128)(2,1)S(1)}, u32[]{:S(2)}, u32[]{:S(2)}) async-start(bf16[32,32,128]{2,1,0:T(8,128)(2,1)} %get-tuple-element.16), calls=%async_computation.1 | async-start | bytes 524288 | tf_op jit(solution)/shard_map/all_to_all | solution.py:901
  41.4 9.6 %collective-permute-start.2 = (bf16[4,128,128]{2,1,0:T(8,128)(2,1)S(1)}, bf16[4,128,128]{2,1,0:T(8,128)(2,1)S(1)}, u32[]{:S(2)}, u32[]{:S(2)}) collective-permute-start(bf16[4,128,128]{2,1,0:T(8,128)(2,1)S(1)} %get-tuple-element.21), channel_id=1, source_target_pairs={{0,1},{1,2},{2,3},{4,5},{5,6},{6,7},{8,9},{9,10},{10,11},{12,13},{... | collective-permute-start | bytes 393224 | tf_op jit(solution)/shard_map/ppermute | solution.py:905
  45.0 6.3 %collective-permute-start.3 = (bf16[4,128,128]{2,1,0:T(8,128)(2,1)S(1)}, bf16[4,128,128]{2,1,0:T(8,128)(2,1)S(1)}, u32[]{:S(2)}, u32[]{:S(2)}) collective-permute-start(bf16[4,128,128]{2,1,0:T(8,128)(2,1)S(1)} %get-tuple-element.22), channel_id=1, source_target_pairs={{1,0},{2,1},{3,2},{5,4},{6,5},{7,6},{9,8},{10,9},{11,10},{13,12},{... | collective-permute-start | bytes 393224 | tf_op jit(solution)/shard_map/ppermute | solution.py:904

commit v2 on v1

--- a/solution.py
+++ b/solution.py
@@ -11,6 +11,7 @@
 SUB = 8
 LANES = 128
 GRANT = 52
+GRANT_ALL = 60
 F32 = jnp.float32
 BF16 = jnp.bfloat16
 VMEM = pl.BlockSpec(memory_space=pltpu.VMEM)
@@ -33,10 +34,9 @@
     return pl.CostEstimate(flops=int(flops), bytes_accessed=int(moved), transcendentals=0)
 
 
-def row_pack_kernel(tracer, speed, first, last, head, tail, sem):
+def edge_copies(tracer, speed, head, tail, sem):
     tracer_count, rows, _ = tracer.shape
     speed_count = speed.shape[0]
-    total = tracer_count + speed_count
     copies = []
     for place, (start, into) in enumerate(((0, head), (rows - SUB, tail))):
         copies.append(
@@ -51,13 +51,13 @@
                 sem.at[place, 1],
             )
         )
-    for copy in copies:
-        copy.start()
+    return copies
+
+
+def pack_edges(total, head, tail, first, last):
     spare = head.shape[0] - total
     for into in (head, tail):
         into[pl.ds(total, spare)] = jnp.zeros((spare, SUB, LANES), F32)
-    for copy in copies:
-        copy.wait()
     for into, out, shift in ((head, first, 0), (tail, last, SUB - NSUB)):
         flat = into.reshape(into.shape[0] * SUB, LANES)
         for row in range(NSUB):
@@ -67,27 +67,10 @@
                 ].astype(BF16)
 
 
-def row_pack(tracer, speed):
-    total = round_up(tracer.shape[0] + speed.shape[0], 16)
-    return pl.pallas_call(
-        row_pack_kernel,
-        out_shape=(shape((NSUB, total, LANES), BF16),) * 2,
-        in_specs=[ANY, ANY],
-        out_specs=(VMEM, VMEM),
-        scratch_shapes=[
-            pltpu.VMEM((total, SUB, LANES), F32),
-            pltpu.VMEM((total, SUB, LANES), F32),
-            pltpu.SemaphoreType.DMA((2, 2)),
-        ],
-        compiler_params=params(GRANT),
-        cost_estimate=cost(1e6, 4e6),
-        name="row_pack",
-    )(tracer, speed)
-
-
 def down_kernel(
-    profile, diffusion, slots, blocks, weight, after, coef_c, coef_g, recip, out,
-    given, mixing, slot, block, held, prof, diff, made_c, made_g, made_r, placed, total, sent, sem, level_sem,
+    profile, diffusion, slots, blocks, weight, tracer, speed, coef_c, coef_g, recip, out, first, last,
+    given, mixing, slot, block, held, prof, diff, made_c, made_g, made_r, placed, total, sent, head, tail,
+    sem, level_sem, edge_sem,
 ):
     fields, levels, columns = profile.shape
     count = columns // LANES
@@ -121,7 +104,8 @@
         pltpu.make_async_copy(slots, slot, sem.at[1]),
         pltpu.make_async_copy(blocks, block, sem.at[2]),
     ]
-    for copy in others:
+    edges = edge_copies(tracer, speed, head, tail, edge_sem)
+    for copy in others + edges:
         copy.start()
     placed[...] = jnp.zeros(placed.shape, F32)
     total[...] = jnp.zeros(total.shape, F32)
@@ -168,7 +152,7 @@
             placed[number, pl.ds(number * width + field, count, stride=rows), :] = value
     for copy in others:
         copy.wait()
-    step = 8
+    step = 32
 
     def body(group, _):
         results = []
@@ -191,16 +175,20 @@
         sent[owner] = total[owner].astype(BF16)
     final = pltpu.make_async_copy(sent, out, sem.at[6])
     final.start()
+    for copy in edges:
+        copy.wait()
+    pack_edges(tracer.shape[0] + speed.shape[0], head, tail, first, last)
     for copy in results_out:
         copy.wait()
     final.wait()
 
 
-def down(profile, diffusion, slots, blocks, weight, after, owners, cap):
+def down(profile, diffusion, slots, blocks, weight, tracer, speed, owners, cap):
     fields, levels, columns = profile.shape
     count = columns // LANES
     rows = cap * (fields + 1)
     padded = round_up(levels, SUB)
+    lines = round_up(tracer.shape[0] + speed.shape[0], 16)
     return pl.pallas_call(
         down_kernel,
         out_shape=(
@@ -208,9 +196,11 @@
             shape((fields, levels * count, LANES)),
             shape((count, LANES)),
             shape((owners, rows, LANES), BF16),
+            shape((NSUB, lines, LANES), BF16),
+            shape((NSUB, lines, LANES), BF16),
         ),
-        in_specs=[ANY] * 5 + [ANY],
-        out_specs=(ANY,) * 4,
+        in_specs=[ANY] * 7,
+        out_specs=(ANY,) * 4 + (VMEM, VMEM),
         scratch_shapes=[
             pltpu.VMEM((fields, padded, columns), F32),
             pltpu.VMEM((padded, columns), F32),
@@ -225,18 +215,21 @@
             pltpu.VMEM((cap, count * rows, LANES), F32),
             pltpu.VMEM((owners, rows, LANES), F32),
             pltpu.VMEM((owners, rows, LANES), BF16),
+            pltpu.VMEM((lines, SUB, LANES), F32),
+            pltpu.VMEM((lines, SUB, LANES), F32),
             pltpu.SemaphoreType.DMA((7,)),
             pltpu.SemaphoreType.DMA((padded // SUB, 2)),
+            pltpu.SemaphoreType.DMA((2, 2)),
         ],
-        compiler_params=params(GRANT),
+        compiler_params=params(GRANT_ALL),
         cost_estimate=cost(1e7, 6e6),
         name="down_sweep",
-    )(profile, diffusion, slots, blocks, weight, after)
+    )(profile, diffusion, slots, blocks, weight, tracer, speed)
 
 
 def flux_kernel(
-    arrived_at, recv_at, coef_at, kind_at, ice_at, tracer, after, later, fluxes_at, answer_at,
-    arrived, recv, coef, kind, ice, surface, fluxes, answer, sem, *, atm, ocn
+    arrived_at, recv_at, coef_at, kind_at, ice_at, tracer, after, fluxes_at, answer_at,
+    arrived, recv, coef, kind, ice, surface, fluxes, answer, narrow, sem, *, atm, ocn
 ):
     loads = [
         pltpu.make_async_copy(source, into, sem.at[place])
@@ -256,8 +249,8 @@
     fields, rows, _ = ice.shape
     width = fields + 1
     slot_total = recv.shape[1]
-    chunk = answer.shape[1]
-    back = arrived.shape[0] // answer.shape[0]
+    owners, chunk, _ = answer.shape
+    back = arrived.shape[0] // owners
     spread = (
         lax.broadcasted_iota(jnp.int32, (slot_total, slot_total * width), 1) // width
         == lax.broadcasted_iota(jnp.int32, (slot_total, slot_total * width), 0)
@@ -269,23 +262,6 @@
     key = row_of.astype(jnp.int32) * width + lane % width
     line = lax.broadcasted_iota(jnp.int32, (width * rows, 1), 0)
     chosen = ((line % rows) * width + line // rows == key).astype(F32)
-    for copy in loads[1:]:
-        copy.wait()
-    summed = jnp.dot(chosen.astype(BF16), arrived[...], preferred_element_type=F32)
-    hold = jnp.where(kind[...] != 0, coef[...], 0.0)
-    over = 1.0 + hold * summed[fields * rows : (fields + 1) * rows]
-    rounded = []
-    for field in range(fields):
-        top = jnp.where(kind[...] == 2, ice[field], surface[field, 0])
-        value = hold * (top - summed[field * rows : (field + 1) * rows]) / over
-        fluxes[field] = value
-        rounded.append(value.astype(BF16).astype(F32))
-    stacked = jnp.concatenate(rounded + [jnp.zeros((rows, LANES), F32)], axis=0).astype(BF16)
-    turned = chosen.T.astype(BF16)
-    returned = jnp.dot(turned, stacked, preferred_element_type=F32)
-    answer[:, pl.ds(0, back), :] = returned.astype(BF16).reshape(answer.shape[0], back, LANES)
-    answer[:, pl.ds(back, chunk - back), :] = jnp.zeros((answer.shape[0], chunk - back, LANES), BF16)
-
     source = lax.broadcasted_iota(jnp.int32, (LANES, 3 * LANES), 0)
     target = lax.broadcasted_iota(jnp.int32, (LANES, 3 * LANES), 1)
     own = source + NSUB
@@ -298,11 +274,30 @@
         | ((target >= 2 * LANES) & (source >= rows - NSUB) & (source < rows))
     )
     place = (fits & ((pos % SUB) * SUB + pos // SUB == target % LANES)).astype(F32).astype(BF16)
+    turned = chosen.T.astype(BF16)
+    chosen = chosen.astype(BF16)
+    for copy in loads[1:]:
+        copy.wait()
+    summed = jnp.dot(chosen, arrived[...], preferred_element_type=F32)
+    hold = jnp.where(kind[...] != 0, coef[...], 0.0)
+    over = 1.0 + hold * summed[fields * rows : (fields + 1) * rows]
+    rounded = []
+    for field in range(fields):
+        top = jnp.where(kind[...] == 2, ice[field], surface[field, 0])
+        value = hold * (top - summed[field * rows : (field + 1) * rows]) / over
+        fluxes[field] = value
+        rounded.append(value.astype(BF16).astype(F32))
+    stacked = jnp.concatenate(rounded + [jnp.zeros((rows, LANES), F32)], axis=0).astype(BF16)
+    returned = jnp.dot(turned, stacked, preferred_element_type=F32)
+    for owner in range(owners):
+        answer[owner, pl.ds(0, back), :] = returned[owner * back : (owner + 1) * back]
+        answer[owner, pl.ds(back, chunk - back), :] = jnp.zeros((chunk - back, LANES), F32)
+
     sides = []
     for field in range(fields):
         tall = jnp.concatenate([rounded[field], jnp.zeros((LANES - rows, LANES), F32)], axis=0)
         sides.append(jnp.dot(tall.T.astype(BF16), place, preferred_element_type=F32))
-    blank = jnp.zeros((chunk - back - fields * NSUB, LANES), F32)
+    gap = jnp.zeros((fields, LANES), F32)
     i = lax.axis_index("atm")
     j = lax.axis_index("ocn")
     for di in (-1, 0, 1):
@@ -318,14 +313,25 @@
                     low = 0 if dj < 0 else LANES - NSUB
                     part = {0: 0, -1: 1, 1: 2}[di] * LANES
                     pieces.append(sides[field][low : low + NSUB, part : part + LANES])
-            tile = jnp.concatenate(pieces + [blank], axis=0).astype(BF16)
+            tile = jnp.concatenate(pieces, axis=0)
+            most = chunk - back
+            filled = []
+            for row in range(most, fields * NSUB):
+                filled += [gap, tile[row : row + 1]]
+            filled.append(jnp.zeros((back - len(filled) // 2 * (fields + 1), LANES), F32))
+            among = jnp.concatenate([part for part in filled if part.shape[0] > 0], axis=0)
 
             @pl.when((i + di >= 0) & (i + di < atm) & (j + dj >= 0) & (j + dj < ocn))
             def _():
-                answer[(i + di) * ocn + j + dj, pl.ds(back, chunk - back), :] = tile
-
+                owner = (i + di) * ocn + j + dj
+                answer[owner, pl.ds(back, most), :] = tile[:most]
+                answer[owner, pl.ds(0, back), :] = answer[owner, pl.ds(0, back), :] + among
+
+    flat = answer.reshape(owners * chunk, LANES)
+    for part in range(0, owners * chunk, 16):
+        narrow[pl.ds(part, 16), :] = flat[pl.ds(part, 16), :].astype(BF16)
     stores = [
-        pltpu.make_async_copy(answer, answer_at, sem.at[6]),
+        pltpu.make_async_copy(narrow, answer_at, sem.at[6]),
         pltpu.make_async_copy(fluxes, fluxes_at, sem.at[7]),
     ]
     for copy in stores:
@@ -334,14 +340,14 @@
         copy.wait()
 
 
-def flux_step(arrived, recv, coef, kind, ice, tracer, after, later, owners, atm, ocn):
+def flux_step(arrived, recv, coef, kind, ice, tracer, after, owners, atm, ocn):
     fields, rows, _ = ice.shape
     back = arrived.shape[0] // owners
-    chunk = back + round_up(fields * NSUB, 16)
+    chunk = back + extra_rows(fields)
     return pl.pallas_call(
         functools.partial(flux_kernel, atm=atm, ocn=ocn),
-        out_shape=(shape(ice.shape), shape((owners, chunk, LANES), BF16)),
-        in_specs=[ANY] * 8,
+        out_shape=(shape(ice.shape), shape((owners * chunk, LANES), BF16)),
+        in_specs=[ANY] * 7,
         out_specs=(ANY, ANY),
         scratch_shapes=[
             pltpu.VMEM(arrived.shape, BF16),
@@ -351,28 +357,31 @@
             pltpu.VMEM(ice.shape, F32),
             pltpu.VMEM((fields, 1, rows, LANES), F32),
             pltpu.VMEM(ice.shape, F32),
-            pltpu.VMEM((owners, chunk, LANES), BF16),
+            pltpu.VMEM((owners, chunk, LANES), F32),
+            pltpu.VMEM((owners * chunk, LANES), BF16),
             pltpu.SemaphoreType.DMA((8,)),
         ],
         compiler_params=params(GRANT),
         cost_estimate=cost(1e7, 1e6),
         name="flux_step",
-    )(arrived, recv, coef, kind, ice, tracer, after, later)
+    )(arrived, recv, coef, kind, ice, tracer, after)
+
+
+def extra_rows(fields):
+    return round_up((fields - 1) * NSUB, SUB)
+
+
+def widen(narrow, wide):
+    flat = wide.reshape(wide.shape[0] * wide.shape[1], LANES)
+    for part in range(0, flat.shape[0], 16):
+        flat[pl.ds(part, 16), :] = narrow[pl.ds(part, 16), :].astype(F32)
 
 
 def spot(column, across):
     return column % across * SUB + column // across
 
 
-def relayout_kernel(
-    tracer, speed, north_at, south_at, out, west, east, north, south, raw, tall, plain, done, sem, fetched, stored
-):
-    halos = [
-        pltpu.make_async_copy(north_at, north, sem.at[0]),
-        pltpu.make_async_copy(south_at, south, sem.at[1]),
-    ]
-    for copy in halos:
-        copy.start()
+def relayout_kernel(tracer, speed, out, west, east, raw, tall, plain, done, fetched, stored):
     tracer_count, rows, _ = tracer.shape
     total = tracer_count + speed.shape[0]
     groups = out.shape[0]
@@ -381,33 +390,20 @@
     wide = out.shape[2]
     across = wide // SUB
 
-    def fetch(group):
-        here = raw.at[pl.ds(group * size, size)]
-        return here, fetched.at[group]
-
     for group in range(groups):
-        into, sem = fetch(group)
         if (group + 1) * size <= tracer_count:
             source = tracer.at[pl.ds(group * size, size)]
         else:
             source = speed.at[pl.ds(group * size - tracer_count, size)]
-        pltpu.make_async_copy(source, into, sem).start()
-    padded_total = north.shape[1]
-    tall[pl.ds(total * high, (padded_total - total) * high), :] = jnp.zeros(
-        ((padded_total - total) * high, LANES), F32
-    )
-    for copy in halos:
-        copy.wait()
-    for row in range(NSUB):
-        for part in range(0, padded_total, 16):
-            for halo, start in ((north, 0), (south, rows + NSUB)):
-                tall[pl.ds(part * high + start + row, 16, stride=high), :] = halo[
-                    row, pl.ds(part, 16), :
-                ].astype(F32)
+        pltpu.make_async_copy(source, raw.at[pl.ds(group * size, size)], fetched.at[group]).start()
+    for part in range(0, tall.shape[0] // high, SUB):
+        for row in list(range(NSUB)) + list(range(rows + NSUB, high)):
+            tall[pl.ds(part * high + row, SUB, stride=high), :] = jnp.zeros((SUB, LANES), F32)
 
     def body(group, _):
-        into, sem = fetch(group)
-        pltpu.make_async_copy(into, into, sem).wait()
+        pltpu.make_async_copy(
+            tracer.at[pl.ds(0, size)], raw.at[pl.ds(group * size, size)], fetched.at[group]
+        ).wait()
         for level in range(size):
             tall[pl.ds(pl.multiple_of(group * size * high, SUB) + level * high + NSUB, rows), :] = raw[
                 group * size + level
@@ -440,7 +436,7 @@
         pltpu.make_async_copy(done.at[group], out.at[group], stored.at[group]).wait()
 
 
-def relayout(tracer, speed, north, south, size):
+def relayout(tracer, speed, size):
     rows = tracer.shape[1]
     total = tracer.shape[0] + speed.shape[0]
     groups = total // size
@@ -453,27 +449,111 @@
             shape((NSUB, slabs, LANES), BF16),
             shape((NSUB, slabs, LANES), BF16),
         ),
-        in_specs=[ANY, ANY, ANY, ANY],
+        in_specs=[ANY] * 2,
         out_specs=(ANY, VMEM, VMEM),
         scratch_shapes=[
-            pltpu.VMEM(north.shape, BF16),
-            pltpu.VMEM(south.shape, BF16),
             pltpu.VMEM((total, rows, LANES), F32),
-            pltpu.VMEM((north.shape[1] * (rows + 2 * NSUB), LANES), F32),
+            pltpu.VMEM((round_up(total, 16) * (rows + 2 * NSUB), LANES), F32),
             pltpu.VMEM((SUB, LANES + 2 * SUB, LANES), F32),
             pltpu.VMEM((groups, SUB, wide, LANES), F32),
-            pltpu.SemaphoreType.DMA((2,)),
             pltpu.SemaphoreType.DMA((groups,)),
             pltpu.SemaphoreType.DMA((groups,)),
         ],
         compiler_params=params(GRANT),
         cost_estimate=cost(1e7, 1.4e7),
         name="relayout",
-    )(tracer, speed, north, south)
+    )(tracer, speed)
+
+
+def halo_kernel(
+    north_at, south_at, west_at, east_at, out, west, east,
+    north, south, own_west, own_east, stacks, plain, done, slim, twice, sem, stored, *, size, coarse
+):
+    groups = out.shape[0]
+    wide = out.shape[1] // NSUB
+    across = wide // SUB
+    loads = [
+        pltpu.make_async_copy(source, into, sem.at[place])
+        for place, (source, into) in enumerate(
+            ((north_at, north), (south_at, south), (west_at, own_west), (east_at, own_east))
+        )
+    ]
+    for copy in loads:
+        copy.start()
+    for copy in loads:
+        copy.wait()
+    for row in range(NSUB):
+        for part in range(0, north.shape[1], 16):
+            for halo, start in ((north, 0), (south, coarse - 1)):
+                stacks[row, pl.ds(part * coarse + start, 16, stride=coarse), :] = halo[
+                    row, pl.ds(part, 16), :
+                ].astype(F32)
+    for group in range(groups):
+        for row in range(NSUB):
+            stack = stacks[row, pl.ds(group * size * coarse, LANES), :]
+            plain[row, pl.ds(SUB, LANES), :] = stack.T
+            for step in range(across):
+                done[group, row, pl.ds(step * SUB, SUB), :] = plain[
+                    row, pl.ds(SUB - NSUB + step, SUB, stride=across), :
+                ]
+        lean = done.reshape(groups, NSUB * wide, LANES)
+        for part in range(0, NSUB * wide, 16):
+            slim[group, pl.ds(part, 16), :] = lean[group, pl.ds(part, 16), :].astype(BF16)
+        pltpu.make_async_copy(slim.at[group], out.at[group], stored.at[group]).start()
+    flat = done.reshape(groups * NSUB * wide, LANES)
+    line = lax.broadcasted_iota(jnp.int32, (16, LANES), 0) % SUB
+    lane = lax.broadcasted_iota(jnp.int32, (16, LANES), 1) % coarse
+    taken = ((line < NSUB) & (lane == 0)) | ((line >= NSUB) & (lane == coarse - 1))
+    for message, own, start in ((west, own_west, NSUB), (east, own_east, wide - 2 * NSUB)):
+        for column in range(NSUB):
+            at = spot(start + column, across)
+            for group in range(groups):
+                few = flat[pl.ds(group * NSUB * wide + at, NSUB, stride=wide), :]
+                twice[pl.ds(group * SUB, NSUB), :] = few
+                twice[pl.ds(group * SUB + NSUB, NSUB), :] = few
+            for part in range(0, message.shape[1], 16):
+                here = pl.ds(part, 16)
+                message[column, here, :] = jnp.where(
+                    taken, twice[here, :], own[column, here, :].astype(F32)
+                ).astype(BF16)
+    for group in range(groups):
+        pltpu.make_async_copy(slim.at[group], out.at[group], stored.at[group]).wait()
+
+
+def halos(north, south, west, east, groups, size, rows):
+    wide = LANES + 2 * NSUB
+    coarse = (rows + 2 * NSUB) // SUB
+    slabs = west.shape[1]
+    return pl.pallas_call(
+        functools.partial(halo_kernel, size=size, coarse=coarse),
+        out_shape=(
+            shape((groups, NSUB * wide, LANES), BF16),
+            shape(west.shape, BF16),
+            shape(east.shape, BF16),
+        ),
+        in_specs=[ANY] * 4,
+        out_specs=(ANY, VMEM, VMEM),
+        scratch_shapes=[
+            pltpu.VMEM(north.shape, BF16),
+            pltpu.VMEM(south.shape, BF16),
+            pltpu.VMEM(west.shape, BF16),
+            pltpu.VMEM(east.shape, BF16),
+            pltpu.VMEM((NSUB, north.shape[1] * coarse, LANES), F32),
+            pltpu.VMEM((NSUB, LANES + 2 * SUB, LANES), F32),
+            pltpu.VMEM((groups, NSUB, wide, LANES), F32),
+            pltpu.VMEM((groups, NSUB * wide, LANES), BF16),
+            pltpu.VMEM((slabs, LANES), F32),
+            pltpu.SemaphoreType.DMA((4,)),
+            pltpu.SemaphoreType.DMA((groups,)),
+        ],
+        compiler_params=params(GRANT),
+        cost_estimate=cost(1e7, 6e6),
+        name="row_halos",
+    )(north, south, west, east)
 
 
 def up_part(
-    answer, out, slot, block, held, made_c, made_g, made_r, sums, solved, final, first, weights, later, out_sem
+    arrived, answer, out, slot, block, held, made_c, made_g, made_r, sums, solved, final, first, weights, later, out_sem
 ):
     fields, levels, columns = out.shape
     count = columns // LANES
@@ -484,13 +564,13 @@
     share = held.shape[0] // parts
     sums[...] = jnp.zeros(sums.shape, F32)
     slot_row = lax.broadcasted_iota(jnp.int32, (rows, LANES), 0) // width
-    step = 8
+    step = 32
 
     def body(group, _):
         results = []
         for inner in range(step):
             at = group * step + inner
-            left = answer[slot[0, at] // cap, pl.ds(0, rows), :]
+            left = answer[slot[0, at] // cap, pl.ds(0, rows), :].astype(BF16)
             results.append(jnp.dot(left, held[at], preferred_element_type=F32))
         for inner in range(step):
             at = group * step + inner
@@ -500,6 +580,7 @@
 
     for copy in first:
         copy.wait()
+    widen(arrived, answer)
     for part in range(parts):
         weights[part].wait()
         lax.fori_loop(part * share // step, (part + 1) * share // step, body, 0)
@@ -537,11 +618,11 @@
 
 
 class Transport:
-    def __init__(self, laid, from_west_at, from_east_at, out, scratch, fields, first, count):
-        self.laid, self.out, self.fields, self.first, self.count = laid, out, fields, first, count
+    def __init__(self, laid, edge, from_west_at, from_east_at, out, scratch, fields, first, count):
+        self.laid, self.edge, self.out, self.fields, self.first, self.count = laid, edge, out, fields, first, count
         (
             self.from_west, self.from_east, self.here, self.there, self.speed, self.along, self.cross,
-            self.halo, self.plain, self.high, self.raw, self.sem, self.fetched, self.stored,
+            self.halo, self.plain, self.high, self.raw, self.edges, self.sem, self.fetched, self.stored,
         ) = scratch
         self.per = laid.shape[0] // (fields + 2)
         self.size = out.shape[0] // (fields * self.per)
@@ -565,11 +646,12 @@
             pltpu.VMEM((SUB + 1, wide, LANES), F32),
             pltpu.VMEM((SUB, wide, LANES), F32),
             pltpu.VMEM((2,) + message_shape, F32),
-            pltpu.VMEM((SUB, LANES + 2 * SUB, LANES), F32),
+            pltpu.VMEM((fields, SUB, LANES + 2 * SUB, LANES), F32),
             pltpu.VMEM((fields, SUB * LANES, LANES), F32),
             pltpu.VMEM((fields * count * size, out_rows, LANES), F32),
+            pltpu.VMEM(((fields + 2) * count, NSUB * wide, LANES), BF16),
             pltpu.SemaphoreType.DMA((2,)),
-            pltpu.SemaphoreType.DMA((fields + 2, count)),
+            pltpu.SemaphoreType.DMA((2, fields + 2, count)),
             pltpu.SemaphoreType.DMA((fields, count)),
         ]
 
@@ -579,7 +661,12 @@
             into = self.here.at[array * self.count + turn]
         else:
             into = self.speed.at[(array - self.fields) * self.count + turn]
-        return pltpu.make_async_copy(self.laid.at[group], into, self.fetched.at[array, turn])
+        return [
+            pltpu.make_async_copy(self.laid.at[group], into, self.fetched.at[0, array, turn]),
+            pltpu.make_async_copy(
+                self.edge.at[group], self.edges.at[array * self.count + turn], self.fetched.at[1, array, turn]
+            ),
+        ]
 
     def store(self, field, turn):
         start = (field * self.per + self.first + turn) * self.size
@@ -591,7 +678,8 @@
 
     def start(self, turn):
         for array in range(self.fields + 2):
-            self.fetch(array, turn).start()
+            for copy in self.fetch(array, turn):
+                copy.start()
         if turn == 0:
             for copy in self.smalls:
                 copy.start()
@@ -605,12 +693,23 @@
 
     def ready(self, turn):
         wide = self.wide
+        coarse = (self.rows + 2 * NSUB) // SUB
+        lane = lax.broadcasted_iota(jnp.int32, (SUB, LANES), 1) % coarse
         for array in range(self.fields + 2):
-            self.fetch(array, turn).wait()
+            for copy in self.fetch(array, turn):
+                copy.wait()
             if array < self.fields:
                 ref, at = self.here, array * self.count + turn
             else:
                 ref, at = self.speed, (array - self.fields) * self.count + turn
+            for part in range(0, NSUB * wide, 16):
+                both = self.edges[array * self.count + turn, pl.ds(part, 16), :].astype(F32)
+                for half in range(2):
+                    value = both[half * SUB : (half + 1) * SUB]
+                    row, step = divmod(part // SUB + half, self.across)
+                    tile = pl.ds(step * SUB, SUB)
+                    for fine, edge in ((row, 0), (row + NSUB, coarse - 1)):
+                        ref[at, fine, tile, :] = jnp.where(lane == edge, value, ref[at, fine, tile, :])
             group = array * self.per + self.first + turn
             flat = ref.reshape(ref.shape[0] * SUB * wide, LANES)
             for side in range(2):
@@ -620,8 +719,8 @@
                         side, column, pl.ds(group * SUB, SUB), :
                     ]
 
-    def force(self, neighbour, fluxes, thin):
-        fields, rows, across, plain = self.fields, self.rows, self.across, self.plain
+    def prepare(self, neighbour, fluxes, thin):
+        fields, rows, plain = self.fields, self.rows, self.plain
         thin[...] = jnp.zeros(thin.shape, F32)
         up_rows = neighbour(-1, 0)
         down_rows = neighbour(1, 0)
@@ -629,7 +728,7 @@
             thin[field, pl.ds(0, NSUB), :] = up_rows[field * NSUB : (field + 1) * NSUB]
             thin[field, pl.ds(NSUB, rows), :] = fluxes[field]
             thin[field, pl.ds(NSUB + rows, NSUB), :] = down_rows[field * NSUB : (field + 1) * NSUB]
-        lane = lax.broadcasted_iota(jnp.int32, (16, LANES), 1)
+        lane = lax.broadcasted_iota(jnp.int32, (fields * NSUB, LANES), 1)
         sides = [sum(neighbour(di, dj) for di in (-1, 0, 1)) for dj in (-1, 1)]
         for fine in range(SUB):
             moved = []
@@ -639,13 +738,18 @@
             for field in range(fields):
                 few = thin[field, pl.ds(fine, SUB, stride=SUB), :]
                 stack = jnp.concatenate([few, jnp.zeros((LANES - SUB, LANES), F32)], axis=0)
-                plain[field, pl.ds(SUB, LANES), :] = stack.T
-                plain[field, pl.ds(SUB - NSUB, NSUB), :] = moved[0][field * NSUB : (field + 1) * NSUB]
-                plain[field, pl.ds(SUB + LANES, NSUB), :] = moved[1][field * NSUB : (field + 1) * NSUB]
-                for step in range(across):
+                plain[field, fine, pl.ds(SUB, LANES), :] = stack.T
+                plain[field, fine, pl.ds(SUB - NSUB, NSUB), :] = moved[0][field * NSUB : (field + 1) * NSUB]
+                plain[field, fine, pl.ds(SUB + LANES, NSUB), :] = moved[1][field * NSUB : (field + 1) * NSUB]
+
+    def force(self):
+        for field in range(self.fields):
+            for fine in range(SUB):
+                for step in range(self.across):
                     at = (field * self.count, fine, pl.ds(step * SUB, SUB))
                     self.here[at] = (
-                        self.here[at] - plain[field, pl.ds(SUB - NSUB + step, SUB, stride=across), :]
+                        self.here[at]
+                        - self.plain[field, fine, pl.ds(SUB - NSUB + step, SUB, stride=self.across), :]
                     )
 
     def faces(self, turn):
@@ -663,7 +767,7 @@
                 lead = (self.count + turn, fine)
                 cross[fine, at, :] = 0.5 * (speed[lead + (at,)] + speed[lead + (after,)])
 
-    def update(self, src, src_at, dst, dst_at):
+    def update(self, src, src_at, dst, dst_at, last_step=False):
         along, cross, fields, across, wide = self.along, self.cross, self.fields, self.across, self.wide
         last = pl.ds(wide - SUB - 1, SUB)
         first = pl.ds(0, SUB)
@@ -695,7 +799,8 @@
                     right = src[src_at[f], fine, after, :]
                     down_flow = down_face * jnp.where(down_pick, value, lower)
                     side_flow = side_face * jnp.where(side_pick, value, right)
-                    dst[dst_at[f], fine, at, :] = (
+                    to = pl.ds(SUB - NSUB + step, SUB, stride=across) if last_step else at
+                    dst[dst_at[f], fine, to, :] = (
                         value + (flow[f] - down_flow) + (carried[f][fine] - side_flow)
                     )
                     flow[f] = down_flow
@@ -709,20 +814,26 @@
         mine = [field * self.count + turn for field in range(fields)]
         spare = list(range(fields))
 
-        def pair(_, carry):
+        def pair(number, carry):
             self.update(self.here, mine, self.there, spare)
-            self.update(self.there, spare, self.here, mine)
+
+            @pl.when(number < NSUB // 2 - 1)
+            def _():
+                self.update(self.there, spare, self.here, mine)
+
+            @pl.when(number == NSUB // 2 - 1)
+            def _():
+                self.update(self.there, spare, plain, spare, last_step=True)
+
             return carry
 
         lax.fori_loop(0, NSUB // 2, pair, 0)
         for field in range(fields):
             lead = field * self.count + turn
             for fine in range(SUB):
-                for step in range(across):
-                    plain[fine, pl.ds(SUB - NSUB + step, SUB, stride=across), :] = self.here[
-                        lead, fine, pl.ds(step * SUB, SUB), :
-                    ]
-                self.high[field, pl.ds(fine, LANES, stride=SUB), :] = plain[fine, pl.ds(SUB, LANES), :].T
+                self.high[field, pl.ds(fine, LANES, stride=SUB), :] = plain[
+                    field, fine, pl.ds(SUB, LANES), :
+                ].T
             base = lead * self.size
             for level in range(self.size):
                 self.raw[base + level] = self.high[field, pl.ds(level * tall + NSUB, self.rows), :]
@@ -736,11 +847,11 @@
 
 def up_kernel(
     answered_at, slots, blocks, weight, coef_c, coef_g, recip,
-    out, answered, slot, block, held, made_c, made_g, made_r, sums, solved, final, sem, out_sem, *, parts
+    out, arrived, answered, slot, block, held, made_c, made_g, made_r, sums, solved, final, sem, out_sem, *, parts
 ):
     share = held.shape[0] // parts
     first = [
-        pltpu.make_async_copy(answered_at, answered, sem.at[0]),
+        pltpu.make_async_copy(answered_at, arrived, sem.at[0]),
         pltpu.make_async_copy(slots, slot, sem.at[1]),
         pltpu.make_async_copy(blocks, block, sem.at[2]),
     ]
@@ -758,14 +869,14 @@
     for copy in first + weights + later:
         copy.start()
     leaving = up_part(
-        answered, out, slot, block, held, made_c, made_g, made_r, sums, solved, final,
+        arrived, answered, out, slot, block, held, made_c, made_g, made_r, sums, solved, final,
         first, weights, later, out_sem,
     )
     for copy in leaving:
         copy.wait()
 
 
-def up(answered, slots, blocks, weight, coef_c, coef_g, recip, levels, cap):
+def up(answered, slots, blocks, weight, coef_c, coef_g, recip, levels, cap, owners):
     fields = coef_g.shape[0]
     count = recip.shape[0]
     rows = cap * (fields + 1)
@@ -778,6 +889,7 @@
         out_specs=ANY,
         scratch_shapes=[
             pltpu.VMEM(answered.shape, BF16),
+            pltpu.VMEM((owners, answered.shape[0] // owners, LANES), F32),
             pltpu.SMEM(slots.shape, jnp.int32),
             pltpu.SMEM(blocks.shape, jnp.int32),
             pltpu.VMEM(weight.shape, BF16),
@@ -797,13 +909,13 @@
 
 
 def advect_kernel(
-    laid, from_west, from_east, fluxes_at, answered_at, out, answered, fluxes, thin, sem, *scratch,
+    laid, edge, from_west, from_east, fluxes_at, answered_at, out, arrived, answered, fluxes, thin, sem, *scratch,
     fields, atm, ocn
 ):
     per = laid.shape[0] // (fields + 2)
-    ocean = Transport(laid, from_west, from_east, out, scratch, fields, 0, per)
+    ocean = Transport(laid, edge, from_west, from_east, out, scratch, fields, 0, per)
     smalls = [
-        pltpu.make_async_copy(answered_at, answered, sem.at[0]),
+        pltpu.make_async_copy(answered_at, arrived, sem.at[0]),
         pltpu.make_async_copy(fluxes_at, fluxes, sem.at[1]),
     ]
     ocean.start(0)
@@ -811,21 +923,26 @@
         copy.start()
     i = lax.axis_index("atm")
     j = lax.axis_index("ocn")
-    back = answered.shape[1] - round_up(fields * NSUB, 16)
 
     def neighbour(di, dj):
         inside = (i + di >= 0) & (i + di < atm) & (j + dj >= 0) & (j + dj < ocn)
         index = jnp.where(inside, (i + di) * ocn + j + dj, 0)
-        value = answered[index, pl.ds(back, answered.shape[1] - back), :].astype(F32)
+        value = answered[index]
+        width = fields + 1
+        back = answered.shape[1] - extra_rows(fields)
+        spare = [value[row : row + 1] for row in range(width - 1, back, width)]
+        value = jnp.concatenate([value[back:]] + spare, axis=0)
         return jnp.where(inside, value, 0.0)
 
+    for copy in smalls:
+        copy.wait()
+    widen(arrived, answered)
+    ocean.prepare(neighbour, fluxes, thin)
     ocean.messages()
     ocean.ready(0)
     for turn in range(1, per):
         ocean.start(turn)
-    for copy in smalls:
-        copy.wait()
-    ocean.force(neighbour, fluxes, thin)
+    ocean.force()
 
     def body(turn, carry):
         ocean.run(turn)
@@ -837,16 +954,17 @@
     ocean.finish()
 
 
-def advect(laid, from_west, from_east, fluxes, answered, rows, size, atm, ocn):
+def advect(laid, edge, from_west, from_east, fluxes, answered, rows, size, atm, ocn):
     fields = fluxes.shape[0]
     per = laid.shape[0] // (fields + 2)
     return pl.pallas_call(
         functools.partial(advect_kernel, fields=fields, atm=atm, ocn=ocn),
         out_shape=shape((fields * per * size, rows, LANES)),
-        in_specs=[ANY] * 5,
+        in_specs=[ANY] * 6,
         out_specs=ANY,
         scratch_shapes=[
             pltpu.VMEM(answered.shape, BF16),
+            pltpu.VMEM((atm * ocn, answered.shape[0] // (atm * ocn), LANES), F32),
             pltpu.VMEM(fluxes.shape, F32),
             pltpu.VMEM((fields, SUB * SUB, LANES), F32),
             pltpu.SemaphoreType.DMA((2,)),
@@ -855,7 +973,7 @@
         compiler_params=params(GRANT),
         cost_estimate=cost(5e7, 1.2e7),
         name="advect",
-    )(laid, from_west, from_east, fluxes, answered)
+    )(laid, edge, from_west, from_east, fluxes, answered)
 
 
 def per_device(
@@ -887,26 +1005,28 @@
         return up, [(target, source) for source, target in up]
 
     forward, backward = neighbours("atm")
-    first, last = row_pack(tracer, speed)
+    coef_c, coef_g, recip, outgoing, first, last = down(
+        atm_state, diffusivity, send_slot, atm_block, remap_weight, tracer, speed, owners, cap
+    )
     south = lax.ppermute(first, "atm", backward)
     north = lax.ppermute(last, "atm", forward)
-    coef_c, coef_g, recip, outgoing = down(
-        atm_state, diffusivity, send_slot, atm_block, remap_weight, first, owners, cap
-    )
     arrived = lax.all_to_all(outgoing, ("atm", "ocn"), split_axis=0, concat_axis=0, tiled=True)
+    laid, own_west, own_east = relayout(tracer, speed, size)
     fluxes, answer = flux_step(
         arrived.reshape(-1, LANES), recv_row, exchange_coef, surface_kind, ice_surface,
-        ocean_tracer, north, south, owners, atm, ocn,
+        ocean_tracer, own_west, owners, atm, ocn,
     )
     answered = lax.all_to_all(answer, ("atm", "ocn"), split_axis=0, concat_axis=0, tiled=True)
-    laid, to_west, to_east = relayout(tracer, speed, north, south, size)
+    edge, to_west, to_east = halos(north, south, own_west, own_east, laid.shape[0], size, rows)
     forward, backward = neighbours("ocn")
     from_east = lax.ppermute(to_west, "ocn", backward)
     from_west = lax.ppermute(to_east, "ocn", forward)
     atm_new = up(
-        answered, send_slot, atm_block, remap_weight, coef_c, coef_g, recip, levels, cap
+        answered, send_slot, atm_block, remap_weight, coef_c, coef_g, recip, levels, cap, owners
     )
-    ocean_new = advect(laid, from_west, from_east, fluxes, answered, rows, size, atm, ocn)
+    ocean_new = advect(
+        laid, edge, from_west, from_east, fluxes, answered, rows, size, atm, ocn
+    )
     return atm_new, ocean_new.reshape(ocean_tracer.shape)
 
 

time: 64.1 us -> 61.5 us (0.959)
  blocking collectives: 15.7 us -> 0 us
  starting transfers between devices: 14.1 us -> 24.8 us
  Pallas kernels: 32.7 us -> 33.9 us
    all_to_all x1 -> x0, blocking collectives: 15.7 us -> none  [per_device(): lax.all_to_all(outgoing, ('atm', 'ocn'), split_axis=0, concat_axis=0, til...]
    all_to_all x0 -> x1, starting transfers between devices: none -> 7.1 us  [per_device(): lax.all_to_all(outgoing, ('atm', 'ocn'), split_axis=0, concat_axis=0, til...]
    all_to_all x1, starting transfers between devices: 3.26 us -> 7.1 us  [per_device(): lax.all_to_all(answer, ('atm', 'ocn'), split_axis=0, concat_axis=0, tiled...]
    ppermute x1, starting transfers between devices: 4.1 us -> 3.31 us  [per_device(): north = lax.ppermute(last, 'atm', forward)]
    pallas_call x1, Pallas kernels: 2.25 us -> 2.9 us  [halos(): pl.pallas_call(functools.partial(halo_kernel, size=size, coarse=coarse),...]
  transfers between devices with their start and end apart: 5 -> 6, of which waited for: 1 -> 3; matrix products, arithmetic and copies ran while one was open for 0% -> 0% of each run, Pallas kernels for 25% -> 25%
where the time goes in v2:
time: 61.5 us; the launch traced here: 60.5 us
  Pallas kernels  33.9 us (55%)
  starting transfers between devices  24.8 us (40%)
  waiting for transfers between devices  0.88 us (1%)
  between operations  0.84 us (1%)
    pallas_call x1, Pallas kernels, advect(): pl.pallas_call(functools.partial(advect_kernel, fields=fields, atm=atm, o...  13 us
    all_to_all x1, starting transfers between devices, per_device(): lax.all_to_all(outgoing, ('atm', 'ocn'), split_axis=0, concat_axis=0, til...  7.1 us
    all_to_all x1, starting transfers between devices, per_device(): lax.all_to_all(answer, ('atm', 'ocn'), split_axis=0, concat_axis=0, tiled...  7.1 us
    pallas_call x1, Pallas kernels, relayout(): pl.pallas_call(relayout_kernel, out_shape=(shape((groups, SUB, wide, LANE...  5.99 us
    pallas_call x1, Pallas kernels, down(): pl.pallas_call(down_kernel, out_shape=(shape(((levels - 1) * count, LANES...  5.85 us
    ppermute x1, starting transfers between devices, per_device(): from_west = lax.ppermute(to_east, 'ocn', forward)  3.95 us
    pallas_call x1, Pallas kernels, up(): pl.pallas_call(functools.partial(up_kernel, parts=parts), out_shape=shape...  3.79 us
    ppermute x1, starting transfers between devices, per_device(): north = lax.ppermute(last, 'atm', forward)  3.31 us
  transfers between devices with their start and end apart: 6, of which 3 were waited for; matrix products, arithmetic and copies ran while one was open for 0% of the time, Pallas kernels for 25%

profile of v2, /device:TPU:1, one launch (start us, length us, event | category | flops | bytes accessed | tf_op | source)
XLA Modules:
  0.0 60.5 jit_solution(10155526900376096625)
XLA Ops:
  0.6 5.9 %down_sweep.1 = (f32[992,128]{1,0:T(8,128)}, f32[3,1008,128]{2,1,0:T(8,128)}, f32[16,128]{1,0:T(8,128)}, bf16[32,16,128]{2,1,0:T(8,128)(2,1)}, bf16[4,384,128]{2...) custom-call(f32[3,63,2048]{2,1,0:T(8,128)} %profile.1, f32[62,2048]{1,0:T(8,128)} %diffusion.1, s32[1,64]{1,0:T(1,128)} %slots.3, ...), custom_call_target="tpu_custom_call" | custom-call | flops 10000000 | bytes 6000000 | tf_op jit(solution)/shard_map/down_sweep/pallas_call | solution.py:192
  6.5 7.1 %all-to-all-start = ((bf16[32,16,128]{2,1,0:T(8,128)(2,1)}), bf16[32,16,128]{2,1,0:T(8,128)(2,1)S(1)}, u32[]{:S(2)}, u32[]{:S(2)}) async-start(bf16[32,16,128]{2,1,0:T(8,128)(2,1)} %get-tuple-element.16), calls=%async_computation | async-start | bytes 262144 | tf_op jit(solution)/shard_map/all_to_all | solution.py:1013
  13.6 3.3 %collective-permute-start = (bf16[4,384,128]{2,1,0:T(8,128)(2,1)}, bf16[4,384,128]{2,1,0:T(8,128)(2,1)S(1)}, u32[]{:S(2)}, u32[]{:S(2)}) collective-permute-start(bf16[4,384,128]{2,1,0:T(8,128)(2,1)} %get-tuple-element.23), channel_id=1, source_target_pairs={{0,4},{4,8},{8,12},{12,16},{16,20},{20,24},{24,28},{1,5},{5,9},{9,... | collective-permute-start | bytes 1179656 | tf_op jit(solution)/shard_map/ppermute | solution.py:1012
  16.9 0.0 copy-start.1
  16.9 0.0 copy-start.2
  16.9 0.0 copy-start.3
  17.0 0.0 copy-start.7
  17.0 1.4 %collective-permute-start.1 = (bf16[4,384,128]{2,1,0:T(8,128)(2,1)}, bf16[4,384,128]{2,1,0:T(8,128)(2,1)S(1)}, u32[]{:S(2)}, u32[]{:S(2)}) collective-permute-start(bf16[4,384,128]{2,1,0:T(8,128)(2,1)} %get-tuple-element.24), channel_id=1, source_target_pairs={{4,0},{8,4},{12,8},{16,12},{20,16},{24,20},{28,24},{5,1},{9,5},{13... | collective-permute-start | bytes 1179656 | tf_op jit(solution)/shard_map/ppermute | solution.py:1011
  18.4 6.0 %relayout.1 = (f32[15,8,136,128]{3,2,1,0:T(8,128)}, bf16[4,128,128]{2,1,0:T(8,128)(2,1)S(1)}, bf16[4,128,128]{2,1,0:T(8,128)(2,1)S(1)}) custom-call(f32[225,32,128]{2,1,0:T(8,128)} %bitcast.10, f32[150,32,128]{2,1,0:T(8,128)} %bitcast.12), custom_call_target="tpu_custom_call" | custom-call | flops 10000000 | bytes 14000000 | tf_op jit(solution)/shard_map/relayout/pallas_call | solution.py:445
  24.4 0.0 all-to-all-done
  24.4 0.0 copy-done.1
  24.4 0.0 copy-done.2
  24.4 0.0 copy-done.3
  24.4 0.0 copy-done.7
  24.4 0.0 copy-start
  24.5 0.0 copy-start.4
  24.5 0.0 copy-start.5
  24.5 0.0 copy-start.6
  24.5 2.4 %flux_step.1 = (f32[3,32,128]{2,1,0:T(8,128)S(1)}, bf16[768,128]{1,0:T(8,128)(2,1)}) custom-call(bf16[512,128]{1,0:T(8,128)(2,1)S(1)} %bitcast.8, s32[1,128]{1,0:T(1,128)S(1)} %copy-done.7, f32[32,128]{1,0:T(8,128)S(1)} %copy-done.2, s32[32,128]{1,0:T(8,128)S(1)} %copy-done.3, f32[3,32,128]{2,1,0:T(8,128)S(1)} %copy-done.1, f32[3,75,32,128]{3,2,1,0:T(8,128)} %tracer.1, ...), custom_call_target="tpu_custom_call" | custom-call | flops 10000000 | bytes 1000000 | tf_op jit(solution)/shard_map/flux_step/pallas_call | solution.py:347
  26.9 7.1 %all-to-all-start.1 = ((bf16[32,24,128]{2,1,0:T(8,128)(2,1)}), bf16[32,24,128]{2,1,0:T(8,128)(2,1)S(1)}, u32[]{:S(2)}, u32[]{:S(2)}) async-start(bf16[32,24,128]{2,1,0:T(8,128)(2,1)} %bitcast.3), calls=%async_computation.1 | async-start | bytes 393216 | tf_op jit(solution)/shard_map/all_to_all | solution.py:1019
  34.0 0.3 collective-permute-done.north_at
  34.3 0.0 collective-permute-done.1.south_at
  34.3 2.9 %row_halos.1 = (bf16[15,544,128]{2,1,0:T(8,128)(2,1)}, bf16[4,128,128]{2,1,0:T(8,128)(2,1)S(1)}, bf16[4,128,128]{2,1,0:T(8,128)(2,1)S(1)}) custom-call(bf16[4,384,128]{2,1,0:T(8,128)(2,1)S(1)} %collective-permute-done.north_at, bf16[4,384,128]{2,1,0:T(8,128)(2,1)S(1)} %collective-permute-done.1.south_at, ...), custom_call_target="tpu_custom_call" | custom-call | flops 10000000 | bytes 6000000 | tf_op jit(solution)/shard_map/row_halos/pallas_call | solution.py:527
  37.2 4.0 %collective-permute-start.2 = (bf16[4,128,128]{2,1,0:T(8,128)(2,1)S(1)}, bf16[4,128,128]{2,1,0:T(8,128)(2,1)S(1)}, u32[]{:S(2)}, u32[]{:S(2)}) collective-permute-start(bf16[4,128,128]{2,1,0:T(8,128)(2,1)S(1)} %get-tuple-element.27), channel_id=1, source_target_pairs={{0,1},{1,2},{2,3},{4,5},{5,6},{6,7},{8,9},{9,10},{10,11},{12,13},{... | collective-permute-start | bytes 393224 | tf_op jit(solution)/shard_map/ppermute | solution.py:1023
  41.2 1.9 %collective-permute-start.3 = (bf16[4,128,128]{2,1,0:T(8,128)(2,1)S(1)}, bf16[4,128,128]{2,1,0:T(8,128)(2,1)S(1)}, u32[]{:S(2)}, u32[]{:S(2)}) collective-permute-start(bf16[4,128,128]{2,1,0:T(8,128)(2,1)S(1)} %get-tuple-element.28), channel_id=1, source_target_pairs={{1,0},{2,1},{3,2},{5,4},{6,5},{7,6},{9,8},{10,9},{11,10},{13,12},{... | collective-permute-start | bytes 393224 | tf_op jit(solution)/shard_map/ppermute | solution.py:1022
  43.1 0.1 all-to-all-done.1
  43.2 0.0 copy-done
  43.2 0.0 copy-done.4
  43.2 0.0 copy-done.5
  43.2 0.0 copy-done.6
  43.2 3.8 %up_sweep.1 = f32[3,63,2048]{2,1,0:T(8,128)} custom-call(bf16[768,128]{1,0:T(8,128)(2,1)S(1)} %bitcast.6, s32[1,64]{1,0:T(1,128)S(1)} %copy-done.5, s32[1,64]{1,0:T(1,128)S(1)} %copy-done.6, bf16[64,128,128]{2,1,0:T(8,128)(2,1)} %weight.3, f32[992,128]{1,0:T(8,128)S(1)} %copy-done, f32[3,1008,128]{2,1,0:T(8,128)} %get-tuple-element.20.coef_g, ...), custom_call_target="tpu_custom_call" | custom-call | flops 10000000 | bytes 6000000 | tf_op jit(solution)/shard_map/up_sweep/pallas_call | solution.py:885
  47.0 0.0 collective-permute-done.2.from_west
  47.0 0.4 collective-permute-done.3.from_east
  47.5 13.0 %advect.1 = f32[225,32,128]{2,1,0:T(8,128)} custom-call(f32[15,8,136,128]{3,2,1,0:T(8,128)} %get-tuple-element.22.laid, bf16[15,544,128]{2,1,0:T(8,128)(2,1)} %get-tuple-element.26.edge, bf16[4,128,128]{2,1,0:T(8,128)(2,1)S(1)} %collective-permute-done.2.from_west, bf16[4,128,128]{2,1,0:T(8,128)(2,1)S(1)} %collective-permute-done.3.from_east, ...), custom_call_target="tpu_custom_call" | custom-call | flops 50000000 | bytes 12000000 | tf_op jit(solution)/shard_map/advect/pallas_call | solution.py:960
Async XLA Ops:
  6.5 17.9 %all-to-all-start = ((bf16[32,16,128]{2,1,0:T(8,128)(2,1)}), bf16[32,16,128]{2,1,0:T(8,128)(2,1)S(1)}, u32[]{:S(2)}, u32[]{:S(2)}) async-start(bf16[32,16,128]{2,1,0:T(8,128)(2,1)} %get-tuple-element.16), calls=%async_computation | async-start | bytes 262144 | tf_op jit(solution)/shard_map/all_to_all | solution.py:1013
  13.6 20.7 %collective-permute-start = (bf16[4,384,128]{2,1,0:T(8,128)(2,1)}, bf16[4,384,128]{2,1,0:T(8,128)(2,1)S(1)}, u32[]{:S(2)}, u32[]{:S(2)}) collective-permute-start(bf16[4,384,128]{2,1,0:T(8,128)(2,1)} %get-tuple-element.23), channel_id=1, source_target_pairs={{0,4},{4,8},{8,12},{12,16},{16,20},{20,24},{24,28},{1,5},{5,9},{9,... | collective-permute-start | bytes 1179656 | tf_op jit(solution)/shard_map/ppermute | solution.py:1012
  16.9 7.5 %copy-start.1 = (f32[3,32,128]{2,1,0:T(8,128)S(1)}, f32[3,32,128]{2,1,0:T(8,128)}, u32[]{:S(2)}) copy-start(f32[3,32,128]{2,1,0:T(8,128)} %ice_at.1) | copy-start | bytes 147460
  16.9 7.5 %copy-start.2 = (f32[32,128]{1,0:T(8,128)S(1)}, f32[32,128]{1,0:T(8,128)}, u32[]{:S(2)}) copy-start(f32[32,128]{1,0:T(8,128)} %coef_at.1) | copy-start | bytes 49156
  16.9 7.5 %copy-start.3 = (s32[32,128]{1,0:T(8,128)S(1)}, s32[32,128]{1,0:T(8,128)}, u32[]{:S(2)}) copy-start(s32[32,128]{1,0:T(8,128)} %kind_at.1) | copy-start | bytes 49156
  17.0 7.5 %copy-start.7 = (s32[1,128]{1,0:T(1,128)S(1)}, s32[1,128]{1,0:T(1,128)}, u32[]{:S(2)}) copy-start(s32[1,128]{1,0:T(1,128)} %recv_at.1) | copy-start | bytes 1540
  17.0 17.4 %collective-permute-start.1 = (bf16[4,384,128]{2,1,0:T(8,128)(2,1)}, bf16[4,384,128]{2,1,0:T(8,128)(2,1)S(1)}, u32[]{:S(2)}, u32[]{:S(2)}) collective-permute-start(bf16[4,384,128]{2,1,0:T(8,128)(2,1)} %get-tuple-element.24), channel_id=1, source_target_pairs={{4,0},{8,4},{12,8},{16,12},{20,16},{24,20},{28,24},{5,1},{9,5},{13... | collective-permute-start | bytes 1179656 | tf_op jit(solution)/shard_map/ppermute | solution.py:1011
  24.4 18.8 %copy-start = (f32[992,128]{1,0:T(8,128)S(1)}, f32[992,128]{1,0:T(8,128)}, u32[]{:S(2)}) copy-start(f32[992,128]{1,0:T(8,128)} %get-tuple-element.19.coef_c) | copy-start | bytes 1523716
  24.5 18.7 %copy-start.4 = (f32[16,128]{1,0:T(8,128)S(1)}, f32[16,128]{1,0:T(8,128)}, u32[]{:S(2)}) copy-start(f32[16,128]{1,0:T(8,128)} %get-tuple-element.21.recip) | copy-start | bytes 24580
  24.5 18.7 %copy-start.5 = (s32[1,64]{1,0:T(1,128)S(1)}, s32[1,64]{1,0:T(1,128)}, u32[]{:S(2)}) copy-start(s32[1,64]{1,0:T(1,128)} %slots.3) | copy-start | bytes 772
  24.5 18.7 %copy-start.6 = (s32[1,64]{1,0:T(1,128)S(1)}, s32[1,64]{1,0:T(1,128)}, u32[]{:S(2)}) copy-start(s32[1,64]{1,0:T(1,128)} %blocks.3) | copy-start | bytes 772
  26.9 16.3 %all-to-all-start.1 = ((bf16[32,24,128]{2,1,0:T(8,128)(2,1)}), bf16[32,24,128]{2,1,0:T(8,128)(2,1)S(1)}, u32[]{:S(2)}, u32[]{:S(2)}) async-start(bf16[32,24,128]{2,1,0:T(8,128)(2,1)} %bitcast.3), calls=%async_computation.1 | async-start | bytes 393216 | tf_op jit(solution)/shard_map/all_to_all | solution.py:1019
  37.2 9.8 %collective-permute-start.2 = (bf16[4,128,128]{2,1,0:T(8,128)(2,1)S(1)}, bf16[4,128,128]{2,1,0:T(8,128)(2,1)S(1)}, u32[]{:S(2)}, u32[]{:S(2)}) collective-permute-start(bf16[4,128,128]{2,1,0:T(8,128)(2,1)S(1)} %get-tuple-element.27), channel_id=1, source_target_pairs={{0,1},{1,2},{2,3},{4,5},{5,6},{6,7},{8,9},{9,10},{10,11},{12,13},{... | collective-permute-start | bytes 393224 | tf_op jit(solution)/shard_map/ppermute | solution.py:1023
  41.2 6.3 %collective-permute-start.3 = (bf16[4,128,128]{2,1,0:T(8,128)(2,1)S(1)}, bf16[4,128,128]{2,1,0:T(8,128)(2,1)S(1)}, u32[]{:S(2)}, u32[]{:S(2)}) collective-permute-start(bf16[4,128,128]{2,1,0:T(8,128)(2,1)S(1)} %get-tuple-element.28), channel_id=1, source_target_pairs={{1,0},{2,1},{3,2},{5,4},{6,5},{7,6},{9,8},{10,9},{11,10},{13,12},{... | collective-permute-start | bytes 393224 | tf_op jit(solution)/shard_map/ppermute | solution.py:1022

commit v3 on v2

--- a/solution.py
+++ b/solution.py
@@ -228,7 +228,7 @@
 
 
 def flux_kernel(
-    arrived_at, recv_at, coef_at, kind_at, ice_at, tracer, after, fluxes_at, answer_at,
+    arrived_at, recv_at, coef_at, kind_at, ice_at, tracer, after, later, fluxes_at, answer_at,
     arrived, recv, coef, kind, ice, surface, fluxes, answer, narrow, sem, *, atm, ocn
 ):
     loads = [
@@ -340,14 +340,14 @@
         copy.wait()
 
 
-def flux_step(arrived, recv, coef, kind, ice, tracer, after, owners, atm, ocn):
+def flux_step(arrived, recv, coef, kind, ice, tracer, after, later, owners, atm, ocn):
     fields, rows, _ = ice.shape
     back = arrived.shape[0] // owners
     chunk = back + extra_rows(fields)
     return pl.pallas_call(
         functools.partial(flux_kernel, atm=atm, ocn=ocn),
         out_shape=(shape(ice.shape), shape((owners * chunk, LANES), BF16)),
-        in_specs=[ANY] * 7,
+        in_specs=[ANY] * 8,
         out_specs=(ANY, ANY),
         scratch_shapes=[
             pltpu.VMEM(arrived.shape, BF16),
@@ -364,7 +364,7 @@
         compiler_params=params(GRANT),
         cost_estimate=cost(1e7, 1e6),
         name="flux_step",
-    )(arrived, recv, coef, kind, ice, tracer, after)
+    )(arrived, recv, coef, kind, ice, tracer, after, later)
 
 
 def extra_rows(fields):
@@ -1014,7 +1014,7 @@
     laid, own_west, own_east = relayout(tracer, speed, size)
     fluxes, answer = flux_step(
         arrived.reshape(-1, LANES), recv_row, exchange_coef, surface_kind, ice_surface,
-        ocean_tracer, own_west, owners, atm, ocn,
+        ocean_tracer, own_west, north, owners, atm, ocn,
     )
     answered = lax.all_to_all(answer, ("atm", "ocn"), split_axis=0, concat_axis=0, tiled=True)
     edge, to_west, to_east = halos(north, south, own_west, own_east, laid.shape[0], size, rows)

time: 61.5 us -> 59.5 us (0.967); the launches traced: 60.5 us -> 59.2 us
  starting transfers between devices: 24.8 us -> 22.8 us
  waiting for transfers between devices: 0.88 us -> 1.56 us
    all_to_all x1, starting transfers between devices: 7.1 us -> 5.6 us  [per_device(): lax.all_to_all(outgoing, ('atm', 'ocn'), split_axis=0, concat_axis=0, til...]
    all_to_all x1, starting transfers between devices: 7.1 us -> 6.34 us  [per_device(): lax.all_to_all(answer, ('atm', 'ocn'), split_axis=0, concat_axis=0, tiled...]
    all_to_all x1, waiting for transfers between devices: 0.09 us -> 0.83 us  [per_device(): lax.all_to_all(answer, ('atm', 'ocn'), split_axis=0, concat_axis=0, tiled...]
    all_to_all x1, waiting for transfers between devices: 0.01 us -> 0.72 us  [per_device(): lax.all_to_all(outgoing, ('atm', 'ocn'), split_axis=0, concat_axis=0, til...]
    ppermute x1, starting transfers between devices: 3.31 us -> 3.96 us  [per_device(): north = lax.ppermute(last, 'atm', forward)]
  transfers between devices with their start and end apart: 6 -> 6, of which waited for: 3 -> 2; matrix products, arithmetic and copies ran while one was open for 0% -> 0% of each run, Pallas kernels for 25% -> 25%
where the time goes in v3:
time: 59.5 us; the launch traced here: 59.2 us
  Pallas kernels  33.9 us (57%)
  starting transfers between devices  22.8 us (38%)
  waiting for transfers between devices  1.56 us (3%)
  between operations  0.84 us (1%)
    pallas_call x1, Pallas kernels, advect(): pl.pallas_call(functools.partial(advect_kernel, fields=fields, atm=atm, o...  13 us
    all_to_all x1, starting transfers between devices, per_device(): lax.all_to_all(answer, ('atm', 'ocn'), split_axis=0, concat_axis=0, tiled...  6.34 us
    pallas_call x1, Pallas kernels, relayout(): pl.pallas_call(relayout_kernel, out_shape=(shape((groups, SUB, wide, LANE...  5.99 us
    pallas_call x1, Pallas kernels, down(): pl.pallas_call(down_kernel, out_shape=(shape(((levels - 1) * count, LANES...  5.85 us
    all_to_all x1, starting transfers between devices, per_device(): lax.all_to_all(outgoing, ('atm', 'ocn'), split_axis=0, concat_axis=0, til...  5.6 us
    ppermute x1, starting transfers between devices, per_device(): north = lax.ppermute(last, 'atm', forward)  3.96 us
    pallas_call x1, Pallas kernels, up(): pl.pallas_call(functools.partial(up_kernel, parts=parts), out_shape=shape...  3.79 us
    ppermute x1, starting transfers between devices, per_device(): from_west = lax.ppermute(to_east, 'ocn', forward)  3.54 us
  transfers between devices with their start and end apart: 6, of which 2 were waited for; matrix products, arithmetic and copies ran while one was open for 0% of the time, Pallas kernels for 25%

profile of v3, /device:TPU:1, one launch (start us, length us, event | category | flops | bytes accessed | tf_op | source)
XLA Modules:
  0.0 59.2 jit_solution(1350076956538994318)
XLA Ops:
  0.6 5.9 %down_sweep.1 = (f32[992,128]{1,0:T(8,128)}, f32[3,1008,128]{2,1,0:T(8,128)}, f32[16,128]{1,0:T(8,128)}, bf16[32,16,128]{2,1,0:T(8,128)(2,1)}, bf16[4,384,128]{2...) custom-call(f32[3,63,2048]{2,1,0:T(8,128)} %profile.1, f32[62,2048]{1,0:T(8,128)} %diffusion.1, s32[1,64]{1,0:T(1,128)} %slots.3, ...), custom_call_target="tpu_custom_call" | custom-call | flops 10000000 | bytes 6000000 | tf_op jit(solution)/shard_map/down_sweep/pallas_call | solution.py:192
  6.5 4.0 %collective-permute-start = (bf16[4,384,128]{2,1,0:T(8,128)(2,1)}, bf16[4,384,128]{2,1,0:T(8,128)(2,1)S(1)}, u32[]{:S(2)}, u32[]{:S(2)}) collective-permute-start(bf16[4,384,128]{2,1,0:T(8,128)(2,1)} %get-tuple-element.18), channel_id=1, source_target_pairs={{0,4},{4,8},{8,12},{12,16},{16,20},{20,24},{24,28},{1,5},{5,9},{9,... | collective-permute-start | bytes 1179656 | tf_op jit(solution)/shard_map/ppermute | solution.py:1012
  10.5 5.6 %all-to-all-start = ((bf16[32,16,128]{2,1,0:T(8,128)(2,1)}), bf16[32,16,128]{2,1,0:T(8,128)(2,1)S(1)}, u32[]{:S(2)}, u32[]{:S(2)}) async-start(bf16[32,16,128]{2,1,0:T(8,128)(2,1)} %get-tuple-element.16), calls=%async_computation | async-start | bytes 262144 | tf_op jit(solution)/shard_map/all_to_all | solution.py:1013
  16.1 0.0 copy-start.1
  16.1 0.0 copy-start.2
  16.1 0.0 copy-start.3
  16.1 0.0 copy-start.7
  16.1 1.4 %collective-permute-start.1 = (bf16[4,384,128]{2,1,0:T(8,128)(2,1)}, bf16[4,384,128]{2,1,0:T(8,128)(2,1)S(1)}, u32[]{:S(2)}, u32[]{:S(2)}) collective-permute-start(bf16[4,384,128]{2,1,0:T(8,128)(2,1)} %get-tuple-element.24), channel_id=1, source_target_pairs={{4,0},{8,4},{12,8},{16,12},{20,16},{24,20},{28,24},{5,1},{9,5},{13... | collective-permute-start | bytes 1179656 | tf_op jit(solution)/shard_map/ppermute | solution.py:1011
  17.6 6.0 %relayout.1 = (f32[15,8,136,128]{3,2,1,0:T(8,128)}, bf16[4,128,128]{2,1,0:T(8,128)(2,1)S(1)}, bf16[4,128,128]{2,1,0:T(8,128)(2,1)S(1)}) custom-call(f32[225,32,128]{2,1,0:T(8,128)} %bitcast.10, f32[150,32,128]{2,1,0:T(8,128)} %bitcast.12), custom_call_target="tpu_custom_call" | custom-call | flops 10000000 | bytes 14000000 | tf_op jit(solution)/shard_map/relayout/pallas_call | solution.py:445
  23.6 0.7 %all-to-all-done = bf16[32,16,128]{2,1,0:T(8,128)(2,1)S(1)} async-done(((bf16[32,16,128]{2,1,0:T(8,128)(2,1)}), bf16[32,16,128]{2,1,0:T(8,128)(2,1)S(1)}, u32[]{:S(2)}, u32[]{:S(2)}) %all-to-all-start) | async-done | bytes 131104 | tf_op jit(solution)/shard_map/all_to_all | solution.py:1013
  24.3 0.0 collective-permute-done.later.north_at
  24.3 0.0 copy-done.1
  24.3 0.0 copy-done.2
  24.3 0.0 copy-done.3
  24.3 0.0 copy-done.7
  24.3 0.0 copy-start
  24.3 0.0 copy-start.4
  24.3 0.0 copy-start.5
  24.3 0.0 copy-start.6
  24.3 2.4 %flux_step.1 = (f32[3,32,128]{2,1,0:T(8,128)S(1)}, bf16[768,128]{1,0:T(8,128)(2,1)}) custom-call(bf16[512,128]{1,0:T(8,128)(2,1)S(1)} %bitcast.8, s32[1,128]{1,0:T(1,128)S(1)} %copy-done.7, f32[32,128]{1,0:T(8,128)S(1)} %copy-done.2, s32[32,128]{1,0:T(8,128)S(1)} %copy-done.3, f32[3,32,128]{2,1,0:T(8,128)S(1)} %copy-done.1, f32[3,75,32,128]{3,2,1,0:T(8,128)} %tracer.1, ...), custom_call_target="tpu_custom_call" | custom-call | flops 10000000 | bytes 1000000 | tf_op jit(solution)/shard_map/flux_step/pallas_call | solution.py:347
  26.7 6.3 %all-to-all-start.1 = ((bf16[32,24,128]{2,1,0:T(8,128)(2,1)}), bf16[32,24,128]{2,1,0:T(8,128)(2,1)S(1)}, u32[]{:S(2)}, u32[]{:S(2)}) async-start(bf16[32,24,128]{2,1,0:T(8,128)(2,1)} %bitcast.3), calls=%async_computation.1 | async-start | bytes 393216 | tf_op jit(solution)/shard_map/all_to_all | solution.py:1019
  33.1 0.0 collective-permute-done.1.south_at
  33.1 2.9 %row_halos.1 = (bf16[15,544,128]{2,1,0:T(8,128)(2,1)}, bf16[4,128,128]{2,1,0:T(8,128)(2,1)S(1)}, bf16[4,128,128]{2,1,0:T(8,128)(2,1)S(1)}) custom-call(bf16[4,384,128]{2,1,0:T(8,128)(2,1)S(1)} %collective-permute-done.later.north_at, bf16[4,384,128]{2,1,0:T(8,128)(2,1)S(1)} %collective-permute-done.1.south_at, ...), custom_call_target="tpu_custom_call" | custom-call | flops 10000000 | bytes 6000000 | tf_op jit(solution)/shard_map/row_halos/pallas_call | solution.py:527
  36.0 3.5 %collective-permute-start.2 = (bf16[4,128,128]{2,1,0:T(8,128)(2,1)S(1)}, bf16[4,128,128]{2,1,0:T(8,128)(2,1)S(1)}, u32[]{:S(2)}, u32[]{:S(2)}) collective-permute-start(bf16[4,128,128]{2,1,0:T(8,128)(2,1)S(1)} %get-tuple-element.27), channel_id=1, source_target_pairs={{0,1},{1,2},{2,3},{4,5},{5,6},{6,7},{8,9},{9,10},{10,11},{12,13},{... | collective-permute-start | bytes 393224 | tf_op jit(solution)/shard_map/ppermute | solution.py:1023
  39.5 1.9 %collective-permute-start.3 = (bf16[4,128,128]{2,1,0:T(8,128)(2,1)S(1)}, bf16[4,128,128]{2,1,0:T(8,128)(2,1)S(1)}, u32[]{:S(2)}, u32[]{:S(2)}) collective-permute-start(bf16[4,128,128]{2,1,0:T(8,128)(2,1)S(1)} %get-tuple-element.28), channel_id=1, source_target_pairs={{1,0},{2,1},{3,2},{5,4},{6,5},{7,6},{9,8},{10,9},{11,10},{13,12},{... | collective-permute-start | bytes 393224 | tf_op jit(solution)/shard_map/ppermute | solution.py:1022
  41.5 0.8 %all-to-all-done.1 = bf16[32,24,128]{2,1,0:T(8,128)(2,1)S(1)} async-done(((bf16[32,24,128]{2,1,0:T(8,128)(2,1)}), bf16[32,24,128]{2,1,0:T(8,128)(2,1)S(1)}, u32[]{:S(2)}, u32[]{:S(2)}) %all-to-all-start.1) | async-done | bytes 196640 | tf_op jit(solution)/shard_map/all_to_all | solution.py:1019
  42.3 0.0 copy-done
  42.3 0.0 copy-done.4
  42.3 0.0 copy-done.5
  42.3 0.0 copy-done.6
  42.3 3.8 %up_sweep.1 = f32[3,63,2048]{2,1,0:T(8,128)} custom-call(bf16[768,128]{1,0:T(8,128)(2,1)S(1)} %bitcast.6, s32[1,64]{1,0:T(1,128)S(1)} %copy-done.5, s32[1,64]{1,0:T(1,128)S(1)} %copy-done.6, bf16[64,128,128]{2,1,0:T(8,128)(2,1)} %weight.3, f32[992,128]{1,0:T(8,128)S(1)} %copy-done, f32[3,1008,128]{2,1,0:T(8,128)} %get-tuple-element.21.coef_g, ...), custom_call_target="tpu_custom_call" | custom-call | flops 10000000 | bytes 6000000 | tf_op jit(solution)/shard_map/up_sweep/pallas_call | solution.py:885
  46.1 0.0 collective-permute-done.2.from_west
  46.1 0.0 collective-permute-done.3.from_east
  46.1 13.0 %advect.1 = f32[225,32,128]{2,1,0:T(8,128)} custom-call(f32[15,8,136,128]{3,2,1,0:T(8,128)} %get-tuple-element.23.laid, bf16[15,544,128]{2,1,0:T(8,128)(2,1)} %get-tuple-element.26.edge, bf16[4,128,128]{2,1,0:T(8,128)(2,1)S(1)} %collective-permute-done.2.from_west, bf16[4,128,128]{2,1,0:T(8,128)(2,1)S(1)} %collective-permute-done.3.from_east, ...), custom_call_target="tpu_custom_call" | custom-call | flops 50000000 | bytes 12000000 | tf_op jit(solution)/shard_map/advect/pallas_call | solution.py:960
Async XLA Ops:
  6.5 17.8 %collective-permute-start = (bf16[4,384,128]{2,1,0:T(8,128)(2,1)}, bf16[4,384,128]{2,1,0:T(8,128)(2,1)S(1)}, u32[]{:S(2)}, u32[]{:S(2)}) collective-permute-start(bf16[4,384,128]{2,1,0:T(8,128)(2,1)} %get-tuple-element.18), channel_id=1, source_target_pairs={{0,4},{4,8},{8,12},{12,16},{16,20},{20,24},{24,28},{1,5},{5,9},{9,... | collective-permute-start | bytes 1179656 | tf_op jit(solution)/shard_map/ppermute | solution.py:1012
  10.5 13.8 %all-to-all-start = ((bf16[32,16,128]{2,1,0:T(8,128)(2,1)}), bf16[32,16,128]{2,1,0:T(8,128)(2,1)S(1)}, u32[]{:S(2)}, u32[]{:S(2)}) async-start(bf16[32,16,128]{2,1,0:T(8,128)(2,1)} %get-tuple-element.16), calls=%async_computation | async-start | bytes 262144 | tf_op jit(solution)/shard_map/all_to_all | solution.py:1013
  16.1 8.2 %copy-start.1 = (f32[3,32,128]{2,1,0:T(8,128)S(1)}, f32[3,32,128]{2,1,0:T(8,128)}, u32[]{:S(2)}) copy-start(f32[3,32,128]{2,1,0:T(8,128)} %ice_at.1) | copy-start | bytes 147460
  16.1 8.2 %copy-start.2 = (f32[32,128]{1,0:T(8,128)S(1)}, f32[32,128]{1,0:T(8,128)}, u32[]{:S(2)}) copy-start(f32[32,128]{1,0:T(8,128)} %coef_at.1) | copy-start | bytes 49156
  16.1 8.2 %copy-start.3 = (s32[32,128]{1,0:T(8,128)S(1)}, s32[32,128]{1,0:T(8,128)}, u32[]{:S(2)}) copy-start(s32[32,128]{1,0:T(8,128)} %kind_at.1) | copy-start | bytes 49156
  16.1 8.2 %copy-start.7 = (s32[1,128]{1,0:T(1,128)S(1)}, s32[1,128]{1,0:T(1,128)}, u32[]{:S(2)}) copy-start(s32[1,128]{1,0:T(1,128)} %recv_at.1) | copy-start | bytes 1540
  16.1 16.9 %collective-permute-start.1 = (bf16[4,384,128]{2,1,0:T(8,128)(2,1)}, bf16[4,384,128]{2,1,0:T(8,128)(2,1)S(1)}, u32[]{:S(2)}, u32[]{:S(2)}) collective-permute-start(bf16[4,384,128]{2,1,0:T(8,128)(2,1)} %get-tuple-element.24), channel_id=1, source_target_pairs={{4,0},{8,4},{12,8},{16,12},{20,16},{24,20},{28,24},{5,1},{9,5},{13... | collective-permute-start | bytes 1179656 | tf_op jit(solution)/shard_map/ppermute | solution.py:1011
  24.3 18.0 %copy-start = (f32[992,128]{1,0:T(8,128)S(1)}, f32[992,128]{1,0:T(8,128)}, u32[]{:S(2)}) copy-start(f32[992,128]{1,0:T(8,128)} %get-tuple-element.20.coef_c) | copy-start | bytes 1523716
  24.3 18.0 %copy-start.4 = (f32[16,128]{1,0:T(8,128)S(1)}, f32[16,128]{1,0:T(8,128)}, u32[]{:S(2)}) copy-start(f32[16,128]{1,0:T(8,128)} %get-tuple-element.22.recip) | copy-start | bytes 24580
  24.3 18.0 %copy-start.5 = (s32[1,64]{1,0:T(1,128)S(1)}, s32[1,64]{1,0:T(1,128)}, u32[]{:S(2)}) copy-start(s32[1,64]{1,0:T(1,128)} %slots.3) | copy-start | bytes 772
  24.3 18.0 %copy-start.6 = (s32[1,64]{1,0:T(1,128)S(1)}, s32[1,64]{1,0:T(1,128)}, u32[]{:S(2)}) copy-start(s32[1,64]{1,0:T(1,128)} %blocks.3) | copy-start | bytes 772
  26.7 15.6 %all-to-all-start.1 = ((bf16[32,24,128]{2,1,0:T(8,128)(2,1)}), bf16[32,24,128]{2,1,0:T(8,128)(2,1)S(1)}, u32[]{:S(2)}, u32[]{:S(2)}) async-start(bf16[32,24,128]{2,1,0:T(8,128)(2,1)} %bitcast.3), calls=%async_computation.1 | async-start | bytes 393216 | tf_op jit(solution)/shard_map/all_to_all | solution.py:1019
  36.0 10.1 %collective-permute-start.2 = (bf16[4,128,128]{2,1,0:T(8,128)(2,1)S(1)}, bf16[4,128,128]{2,1,0:T(8,128)(2,1)S(1)}, u32[]{:S(2)}, u32[]{:S(2)}) collective-permute-start(bf16[4,128,128]{2,1,0:T(8,128)(2,1)S(1)} %get-tuple-element.27), channel_id=1, source_target_pairs={{0,1},{1,2},{2,3},{4,5},{5,6},{6,7},{8,9},{9,10},{10,11},{12,13},{... | collective-permute-start | bytes 393224 | tf_op jit(solution)/shard_map/ppermute | solution.py:1023
  39.5 6.6 %collective-permute-start.3 = (bf16[4,128,128]{2,1,0:T(8,128)(2,1)S(1)}, bf16[4,128,128]{2,1,0:T(8,128)(2,1)S(1)}, u32[]{:S(2)}, u32[]{:S(2)}) collective-permute-start(bf16[4,128,128]{2,1,0:T(8,128)(2,1)S(1)} %get-tuple-element.28), channel_id=1, source_target_pairs={{1,0},{2,1},{3,2},{5,4},{6,5},{7,6},{9,8},{10,9},{11,10},{13,12},{... | collective-permute-start | bytes 393224 | tf_op jit(solution)/shard_map/ppermute | solution.py:1022
